TPU v7x, 512 devices: a whole 4x8x8 slice. The times are simulated.
512 devices in a mesh: dp: 8 (over x, core), expert: 64 (over z, y).
Axes of the slice: x: 4, y: 8, z: 8, core: 2. Of those that a mesh axis runs over, the one named last changes fastest.
Arguments:
- tokens: bfloat16 [65536, 2048], P(('dp', 'expert')), may hold values from -6 to 6
- routes: int32 [65536, 2], P(('dp', 'expert')), may hold values from 0 to 63, all different within a row; in each aligned block of 128 rows (0 to 127, 128 to 255, ...) at most 6 rows name the same one
- route_gates: bfloat16 [65536, 2], P(('dp', 'expert')), may hold values from 0.049804688 to 0.5
- out_grad: bfloat16 [65536, 2048], P(('dp', 'expert')), may hold values from -3 to 3
- w_gate: bfloat16 [64, 2048, 384], P('expert', 'dp'), may hold values from -0.125 to 0.125
- w_up: bfloat16 [64, 2048, 384], P('expert', 'dp'), may hold values from -0.125 to 0.125
- w_down: bfloat16 [64, 384, 2048], P('expert', 'dp'), may hold values from -0.3125 to 0.3125
Outputs:
- token_grad: bfloat16 [65536, 2048], P(('dp', 'expert'))
- gate_grad: bfloat16 [65536, 2], P(('dp', 'expert'))
- down_grad: bfloat16 [64, 384, 2048], P('expert', 'dp')
Inputs may be any that keep to these rules, and one draw needn't show every extreme that they name: `routes`: each row names 2 different experts. Within each aligned block of 128 rows (the tokens of one device) no expert is named more than 6 times, and in some block some expert is named exactly 6 times.
All inputs are finite; a program needn't handle non-finite values.
Results may differ from a plain program's by a relative error of at most 0.019.
Values may be sent and summed in bfloat16 or wider, within the bound.
No kernel may reach another device: no remote copies, remote signals or barrier semaphores. Data moves between devices by JAX's collectives and lax.ppermute only.
A program may use at most 64 MiB of HBM per device.

v0:
```python
import jax
import jax.numpy as jnp
from jax import lax
from jax.sharding import PartitionSpec as P

CONTRACT_LAST = (((1,), (1,)), ((), ()))
CONTRACT_FIRST = (((0,), (0,)), ((), ()))


def slot_tables(routes, experts, capacity):
    tok_count, fan_out = routes.shape
    flat_ids = routes.reshape(-1)
    matches = (flat_ids[:, None] == jnp.arange(experts, dtype=jnp.int32)[None, :]).astype(jnp.int32)
    before = jnp.cumsum(matches, axis=0) - matches
    ranking = jnp.sum(before * matches, axis=1)
    target = flat_ids * capacity + ranking
    placing = (target[None, :] == jnp.arange(experts * capacity, dtype=jnp.int32)[:, None]).astype(
        jnp.bfloat16
    )
    per_token = placing.reshape(experts * capacity, tok_count, fan_out).sum(axis=2)
    return (placing, per_token)


def by_blocks(function, operands, block_rows):
    shaped = tuple((operand.reshape((-1, block_rows) + operand.shape[1:]) for operand in operands))
    result = lax.map(lambda pieces: function(*pieces), shaped)
    return result.reshape((-1,) + result.shape[2:])


def local(tokens, routes, route_gates, out_grad, w_gate, w_up, w_down):
    experts = w_gate.shape[0] * lax.axis_size("expert")
    tok_count, fan_out = routes.shape
    model_dim = tokens.shape[1]
    capacity = 3 * tok_count * fan_out // (2 * experts)
    slot_count = experts * capacity
    block_rows = slot_count
    for candidate in (512, 384, 256, 192, 128):
        if slot_count % candidate == 0 and block_rows == slot_count and (slot_count > candidate):
            block_rows = candidate
    placing, per_token = slot_tables(routes, experts, capacity)
    slot_inputs = jnp.dot(per_token, tokens, preferred_element_type=jnp.float32).astype(
        jnp.bfloat16
    )
    slot_inputs = slot_inputs.reshape(experts, capacity, model_dim)
    slot_grads = jnp.dot(per_token, out_grad, preferred_element_type=jnp.float32).astype(
        jnp.bfloat16
    )
    slot_grads = slot_grads.reshape(experts, capacity, model_dim)
    slot_gates = jnp.dot(placing, route_gates.reshape(-1), preferred_element_type=jnp.float32)
    slot_gates = slot_gates.astype(jnp.bfloat16).reshape(experts, capacity)
    gate_full, up_full, down_full = (
        lax.all_gather(w_gate, "dp", axis=1, tiled=True),
        lax.all_gather(w_up, "dp", axis=1, tiled=True),
        lax.all_gather(w_down, "dp", axis=1, tiled=True),
    )
    gate_mat = gate_full[0]
    up_mat = up_full[0]
    down_mat = down_full[0]
    recv_inputs = lax.all_to_all(slot_inputs, "expert", split_axis=0, concat_axis=0, tiled=True)
    inputs_flat = recv_inputs.reshape(slot_count, model_dim)
    pre_gate = jnp.dot(inputs_flat, gate_mat, preferred_element_type=jnp.float32)
    pre_up = jnp.dot(inputs_flat, up_mat, preferred_element_type=jnp.float32)
    squash = jax.nn.sigmoid(pre_gate)
    activated = pre_gate * squash
    hidden = (activated * pre_up).astype(jnp.bfloat16)
    expert_out = by_blocks(
        lambda rows_in: jnp.dot(rows_in, down_mat, preferred_element_type=jnp.float32).astype(
            jnp.bfloat16
        ),
        (hidden,),
        block_rows,
    )
    recv_grads, recv_gates = (
        lax.all_to_all(slot_grads, "expert", split_axis=0, concat_axis=0, tiled=True),
        lax.all_to_all(slot_gates, "expert", split_axis=0, concat_axis=0, tiled=True),
    )
    grads_flat = recv_grads.reshape(slot_count, model_dim)
    scaled = (
        recv_gates.reshape(slot_count, 1).astype(jnp.float32) * grads_flat.astype(jnp.float32)
    ).astype(jnp.bfloat16)
    hidden_grad = lax.dot_general(
        scaled, down_mat, CONTRACT_LAST, preferred_element_type=jnp.float32
    )
    grad_gate = (hidden_grad * pre_up * squash * (1.0 + pre_gate * (1.0 - squash))).astype(
        jnp.bfloat16
    )
    grad_upper = (hidden_grad * activated).astype(jnp.bfloat16)

    def input_rows(gate_rows, upper_rows):
        summed = lax.dot_general(
            gate_rows, gate_mat, CONTRACT_LAST, preferred_element_type=jnp.float32
        )
        summed = summed + lax.dot_general(
            upper_rows, up_mat, CONTRACT_LAST, preferred_element_type=jnp.float32
        )
        return summed.astype(jnp.bfloat16)

    input_part = by_blocks(input_rows, (grad_gate, grad_upper), block_rows)
    down_total = lax.psum_scatter(
        lax.dot_general(hidden, scaled, CONTRACT_FIRST, preferred_element_type=jnp.float32).astype(
            jnp.bfloat16
        ),
        "dp",
        scatter_dimension=0,
        tiled=True,
    )
    down_grad = down_total[None]
    part_slots = input_part.reshape(experts, capacity, model_dim)
    out_slots = expert_out.reshape(experts, capacity, model_dim)
    back_inputs, back_outputs = (
        lax.all_to_all(part_slots, "expert", split_axis=0, concat_axis=0, tiled=True),
        lax.all_to_all(out_slots, "expert", split_axis=0, concat_axis=0, tiled=True),
    )
    each_output = lax.dot_general(
        placing,
        back_outputs.reshape(slot_count, model_dim),
        CONTRACT_FIRST,
        preferred_element_type=jnp.float32,
    ).astype(jnp.bfloat16)
    each_output = each_output.reshape(tok_count, fan_out, model_dim)
    gate_grad = jnp.einsum("tkd,td->tk", each_output, out_grad, preferred_element_type=jnp.float32)
    gate_grad = gate_grad.astype(jnp.bfloat16)
    token_grad = lax.dot_general(
        per_token,
        back_inputs.reshape(slot_count, model_dim),
        CONTRACT_FIRST,
        preferred_element_type=jnp.float32,
    ).astype(jnp.bfloat16)
    return (token_grad, gate_grad, down_grad)


def solution(mesh):
    placed = (
        P(("dp", "expert"), None),
        P(("dp", "expert"), None),
        P(("dp", "expert"), None),
        P(("dp", "expert"), None),
        P("expert", "dp", None),
        P("expert", "dp", None),
        P("expert", "dp", None),
    )
    return jax.shard_map(
        local,
        mesh=mesh,
        in_specs=placed,
        out_specs=(P(("dp", "expert"), None), P(("dp", "expert"), None), P("expert", "dp", None)),
        check_vma=False,
    )
```

profile of v0, /device:TPU:6, one launch (start us, length us, event | category | flops | bytes accessed | tf_op | source)
XLA Modules:
  0.0 297.5 jit_solution(18108683827901182416)
XLA Ops:
  7.2 0.7 all-gather.4.cloned.1.call-update
  7.9 0.8 copy.32
  8.7 0.1 eq.49
  8.8 0.1 eq.45
  9.0 0.6 reduce-window.6
  9.6 0.2 slice_reduce_fusion
  9.8 0.8 copy.36
  10.6 0.1 reshape.113
  10.8 0.1 fusion.25
  10.9 0.2 convolution_reduce_fusion
  11.1 0.8 all_to_all.24
  11.9 16.6 %all-to-all-start = ((bf16[64,1,6]{2,1,0:T(2,128)(2,1)}), bf16[64,1,6]{2,1,0:T(2,128)(2,1)S(1)}, u32[]{:S(2)}, u32[]{:S(2)}) async-start(bf16[64,1,6]{2,1,0:T(2,128)(2,1)} %all_to_all.24), calls=%async_computation | async-start | bytes 65536 | tf_op jit(solution)/shard_map/all_to_all | solution.py:75
  28.5 0.1 reduce_sum.24
  28.6 0.1 copy.35
  28.7 0.7 multiply_add_fusion.1
  29.4 0.1 fusion.20
  29.5 0.6 convolution_convert_fusion.3
  30.0 1.6 reshape.101
  31.6 8.8 %all-to-all-done = bf16[64,1,6]{2,1,0:T(2,128)(2,1)S(1)} async-done(((bf16[64,1,6]{2,1,0:T(2,128)(2,1)}), bf16[64,1,6]{2,1,0:T(2,128)(2,1)S(1)}, u32[]{:S(2)}, u32[]{:S(2)}) %all-to-all-start) | async-done | bytes 800 | tf_op jit(solution)/shard_map/all_to_all | solution.py:75
  40.4 4.7 %all-to-all-start.1 = ((bf16[64,6,2048]{2,1,0:T(8,128)(2,1)}), bf16[64,6,2048]{2,1,0:T(8,128)(2,1)S(1)}, u32[]{:S(2)}, u32[]{:S(2)}) async-start(bf16[64,6,2048]{2,1,0:T(8,128)(2,1)} %reshape.101), calls=%async_computation.1 | async-start | bytes 4194304 | tf_op jit(solution)/shard_map/all_to_all | solution.py:74
  45.1 0.0 all-gather.8.cloned.1.call-start
  45.2 0.7 all-gather.8.cloned.1.call-update
  45.9 1.7 convolution_convert_fusion.2
  47.6 3.7 %reshape.102 = bf16[64,6,2048]{2,1,0:T(8,128)(2,1)} reshape(bf16[384,2048]{1,0:T(8,128)(2,1)} %convolution_convert_fusion.2) | data formatting | bytes 3145728 | tf_op jit(solution)/shard_map/reshape | solution.py:44
  51.2 45.5 %all-to-all-done.1 = bf16[64,6,2048]{2,1,0:T(8,128)(2,1)S(1)} async-done(((bf16[64,6,2048]{2,1,0:T(8,128)(2,1)}), bf16[64,6,2048]{2,1,0:T(8,128)(2,1)S(1)}, u32[]{:S(2)}, u32[]{:S(2)}) %all-to-all-start.1) | async-done | bytes 1572896 | tf_op jit(solution)/shard_map/all_to_all | solution.py:74
  96.7 6.7 %all-to-all-start.2 = ((bf16[64,6,2048]{2,1,0:T(8,128)(2,1)}), bf16[64,6,2048]{2,1,0:T(8,128)(2,1)}, u32[]{:S(2)}, u32[]{:S(2)}) async-start(bf16[64,6,2048]{2,1,0:T(8,128)(2,1)} %reshape.102), calls=%async_computation.2 | async-start | bytes 4194304 | tf_op jit(solution)/shard_map/all_to_all | solution.py:59
  103.5 0.0 all-gather.6.cloned.1.call-start
  103.5 0.7 all-gather.6.cloned.1.call-update
  104.2 1.8 multiply_convert_fusion
  106.0 3.7 %convert_element_type.92 = bf16[384,2048]{1,0:T(8,128)(2,1)} reshape(bf16[64,6,2048]{2,1,0:T(8,128)(2,1)} %multiply_convert_fusion) | data formatting | bytes 3145728 | tf_op jit(solution)/shard_map/convert_element_type | solution.py:80
  109.7 44.0 %all-to-all-done.2 = bf16[64,6,2048]{2,1,0:T(8,128)(2,1)} async-done(((bf16[64,6,2048]{2,1,0:T(8,128)(2,1)}), bf16[64,6,2048]{2,1,0:T(8,128)(2,1)}, u32[]{:S(2)}, u32[]{:S(2)}) %all-to-all-start.2) | async-done | bytes 1572896 | tf_op jit(solution)/shard_map/all_to_all | solution.py:59
  153.7 2.6 reshape.103
  156.4 3.7 %fusion.31 = f32[384,384]{1,0:T(8,128)} fusion(bf16[384,2048]{1,0:T(8,128)(2,1)} %convert_element_type.92, bf16[1,384,2048]{2,1,0:T(8,128)(2,1)} %all-gather.4.cloned.1.call-done), kind=kOutput, calls=%fused_computation.55 | convolution fusion | flops 603979776 | bytes 3735552 | tf_op jit(solution)/shard_map/dot_general | solution.py:81
  160.1 3.2 %fusion.27 = f32[384,384]{1,0:T(8,128)} fusion(bf16[384,2048]{1,0:T(8,128)(2,1)S(1)} %reshape.103, bf16[1,2048,384]{2,1,0:T(8,128)(2,1)} %all-gather.8.cloned.1.call-done), kind=kOutput, calls=%fused_computation.51 | convolution fusion | flops 603979776 | bytes 3735552 | tf_op jit(solution)/shard_map/dot_general | solution.py:61
  163.3 2.8 multiply_convert_fusion.3
  166.2 1.3 broadcast.34.clone.1
  167.5 0.6 copy-done.1
  168.1 2.9 while.21
  168.1 1.4 fusion.66
  169.6 1.5 fusion.66
  171.0 3.7 %reshape_reshape.7 = bf16[64,6,2048]{2,1,0:T(8,128)(2,1)} reshape(bf16[2,192,2048]{2,1,0:T(8,128)(2,1)} %get-tuple-element.58) | data formatting | bytes 3145728 | tf_op jit(solution)/shard_map/reshape;reshape | solution.py:109
  174.7 6.8 %all-to-all-start.4 = ((bf16[64,6,2048]{2,1,0:T(8,128)(2,1)}), bf16[64,6,2048]{2,1,0:T(8,128)(2,1)}, u32[]{:S(2)}, u32[]{:S(2)}) async-start(bf16[64,6,2048]{2,1,0:T(8,128)(2,1)} %reshape_reshape.7), calls=%async_computation.4 | async-start | bytes 4194304 | tf_op jit(solution)/shard_map/all_to_all | solution.py:112
  181.5 0.1 convert_reduce_fusion
  181.6 0.1 reshape.111
  181.8 1.4 broadcast.34.clone
  183.2 7.5 %while.20 = (s32[]{:T(128)}, bf16[2,192,2048]{2,1,0:T(8,128)(2,1)}, bf16[2,192,384]{2,1,0:T(8,128)(2,1)S(1)}, bf16[2048,384]{1,0:T(8,128)(2,1)}, bf16[2,192,384]...) while((s32[]{:T(128)}, bf16[2,192,2048]{2,1,0:T(8,128)(2,1)}, ...), condition=%wide.region_5.6_spmd, body=%wide.region_4.5_spmd.sunk | while | flops 604766208 | bytes 7373905 | solution.py:26
  183.2 2.1 fusion.62
  185.3 1.6 fusion.63
  186.9 2.1 fusion.62
  189.0 1.6 fusion.63
  190.6 3.9 %reshape_reshape.6 = bf16[64,6,2048]{2,1,0:T(8,128)(2,1)} reshape(bf16[2,192,2048]{2,1,0:T(8,128)(2,1)} %get-tuple-element.57) | data formatting | bytes 3145728 | tf_op jit(solution)/shard_map/reshape;reshape | solution.py:108
  194.5 1.9 reshape.112
  196.4 34.3 %all-to-all-done.4 = bf16[64,6,2048]{2,1,0:T(8,128)(2,1)} async-done(((bf16[64,6,2048]{2,1,0:T(8,128)(2,1)}), bf16[64,6,2048]{2,1,0:T(8,128)(2,1)}, u32[]{:S(2)}, u32[]{:S(2)}) %all-to-all-start.4) | async-done | bytes 1572896 | tf_op jit(solution)/shard_map/all_to_all | solution.py:112
  230.7 6.8 %all-to-all-start.3 = ((bf16[64,6,2048]{2,1,0:T(8,128)(2,1)}), bf16[64,6,2048]{2,1,0:T(8,128)(2,1)S(1)}, u32[]{:S(2)}, u32[]{:S(2)}) async-start(bf16[64,6,2048]{2,1,0:T(8,128)(2,1)} %reshape_reshape.6), calls=%async_computation.3 | async-start | bytes 4194304 | tf_op jit(solution)/shard_map/all_to_all | solution.py:111
  237.5 0.0 reduce-scatter.2.cloned.1.call-start
  237.5 4.2 %convolution_convert_fusion.1 = bf16[384,2048]{1,0:T(8,128)(2,1)} fusion(bf16[384,384]{1,0:T(8,128)(2,1)S(1)} %bitcast.93, f32[384,2048]{1,0:T(8,128)} %reshape.112, f32[384]{0:T(512)S(1)} %reshape.111), kind=kOutput, calls=%fused_computation.19 | convolution fusion | flops 606339072 | bytes 5015040 | tf_op jit(solution)/shard_map/dot_general | solution.py:100
  241.7 3.7 %reshape.108 = bf16[384,2048]{1,0:T(8,128)(2,1)} reshape(bf16[64,6,2048]{2,1,0:T(8,128)(2,1)} %all-to-all-done.4) | data formatting | bytes 3145728 | tf_op jit(solution)/shard_map/reshape | solution.py:116
  245.5 3.1 %convolution_convert_fusion.4 = bf16[256,2048]{1,0:T(8,128)(2,1)} fusion(bf16[384,2048]{1,0:T(8,128)(2,1)} %reshape.108, s32[256]{0:T(256)S(1)} %multiply_add_fusion), kind=kOutput, calls=%fused_computation.22 | convolution fusion | flops 403275776 | bytes 2622464 | tf_op jit(solution)/shard_map/dot_general | solution.py:114
  248.6 2.5 reshape.109
  251.1 3.5 %fusion.16 = bf16[128,1,2]{2,1,0:T(2,128)(2,1)S(1)} fusion(bf16[128,2,2048]{2,1,0:T(2,128)(2,1)} %reshape.109, bf16[128,2048,1]{1,0,2:T(8,128)(2,1)S(1)} %bitcast.88), kind=kOutput, calls=%fused_computation.26 | convolution fusion | flops 1048576 | bytes 1573376 | tf_op jit(solution)/shard_map/tkd,td->tk/dot_general | solution.py:121
  254.7 0.6 copy.39
  255.3 31.6 %all-to-all-done.3 = bf16[64,6,2048]{2,1,0:T(8,128)(2,1)S(1)} async-done(((bf16[64,6,2048]{2,1,0:T(8,128)(2,1)}), bf16[64,6,2048]{2,1,0:T(8,128)(2,1)S(1)}, u32[]{:S(2)}, u32[]{:S(2)}) %all-to-all-start.3) | async-done | bytes 1572896 | tf_op jit(solution)/shard_map/all_to_all | solution.py:111
  286.9 1.4 reshape.106
  288.3 2.7 convolution_convert_fusion.5
  (22 shorter events, 0.2 us)
Async XLA Ops:
  7.2 22.3 %copy-start = (bf16[128,2048]{1,0:T(8,128)(2,1)S(1)}, bf16[128,2048]{1,0:T(8,128)(2,1)}, u32[]{:S(2)}) copy-start(bf16[128,2048]{1,0:T(8,128)(2,1)} %param.14) | copy-start | bytes 1572868
  7.2 149.2 %all-gather.4.cloned.1.call-start = ((), (), s32[]{:S(2)}) async-start(), calls=%async_computation.6 | async-start | bytes 1769472 | tf_op jit(solution)/shard_map/all_gather | solution.py:54
  11.9 28.5 %all-to-all-start = ((bf16[64,1,6]{2,1,0:T(2,128)(2,1)}), bf16[64,1,6]{2,1,0:T(2,128)(2,1)S(1)}, u32[]{:S(2)}, u32[]{:S(2)}) async-start(bf16[64,1,6]{2,1,0:T(2,128)(2,1)} %all_to_all.24), calls=%async_computation | async-start | bytes 65536 | tf_op jit(solution)/shard_map/all_to_all | solution.py:75
  31.6 14.2 %copy-start.5 = (bf16[128,2048]{1,0:T(8,128)(2,1)S(1)}, bf16[128,2048]{1,0:T(8,128)(2,1)}, u32[]{:S(2)}) copy-start(bf16[128,2048]{1,0:T(8,128)(2,1)} %param.11) | copy-start | bytes 1572868
  40.4 56.3 %all-to-all-start.1 = ((bf16[64,6,2048]{2,1,0:T(8,128)(2,1)}), bf16[64,6,2048]{2,1,0:T(8,128)(2,1)S(1)}, u32[]{:S(2)}, u32[]{:S(2)}) async-start(bf16[64,6,2048]{2,1,0:T(8,128)(2,1)} %reshape.101), calls=%async_computation.1 | async-start | bytes 4194304 | tf_op jit(solution)/shard_map/all_to_all | solution.py:74
  45.1 115.0 %all-gather.8.cloned.1.call-start = ((), (), s32[]{:S(2)}) async-start(), calls=%async_computation.8 | async-start | bytes 1769472 | tf_op jit(solution)/shard_map/all_gather | solution.py:52
  96.7 7.5 %copy-start.3 = (bf16[64,6,2048]{2,1,0:T(8,128)(2,1)}, bf16[64,6,2048]{2,1,0:T(8,128)(2,1)S(1)}, u32[]{:S(2)}) copy-start(bf16[64,6,2048]{2,1,0:T(8,128)(2,1)S(1)} %all-to-all-done.1) | copy-start | bytes 4718596
  96.7 57.0 %all-to-all-start.2 = ((bf16[64,6,2048]{2,1,0:T(8,128)(2,1)}), bf16[64,6,2048]{2,1,0:T(8,128)(2,1)}, u32[]{:S(2)}, u32[]{:S(2)}) async-start(bf16[64,6,2048]{2,1,0:T(8,128)(2,1)} %reshape.102), calls=%async_computation.2 | async-start | bytes 4194304 | tf_op jit(solution)/shard_map/all_to_all | solution.py:59
  103.5 59.9 %all-gather.6.cloned.1.call-start = ((), (), s32[]{:S(2)}) async-start(), calls=%async_computation.7 | async-start | bytes 1769472 | tf_op jit(solution)/shard_map/all_gather | solution.py:53
  166.2 2.0 copy-start.1
  174.7 55.9 %all-to-all-start.4 = ((bf16[64,6,2048]{2,1,0:T(8,128)(2,1)}), bf16[64,6,2048]{2,1,0:T(8,128)(2,1)}, u32[]{:S(2)}, u32[]{:S(2)}) async-start(bf16[64,6,2048]{2,1,0:T(8,128)(2,1)} %reshape_reshape.7), calls=%async_computation.4 | async-start | bytes 4194304 | tf_op jit(solution)/shard_map/all_to_all | solution.py:112
  181.5 1.6 copy-start.2
  190.6 3.9 %copy-start.4 = (bf16[64,6,2048]{2,1,0:T(8,128)(2,1)S(1)}, bf16[64,6,2048]{2,1,0:T(8,128)(2,1)}, u32[]{:S(2)}) copy-start(bf16[64,6,2048]{2,1,0:T(8,128)(2,1)} %copy-done.3) | copy-start | bytes 4718596
  230.7 56.2 %all-to-all-start.3 = ((bf16[64,6,2048]{2,1,0:T(8,128)(2,1)}), bf16[64,6,2048]{2,1,0:T(8,128)(2,1)S(1)}, u32[]{:S(2)}, u32[]{:S(2)}) async-start(bf16[64,6,2048]{2,1,0:T(8,128)(2,1)} %reshape_reshape.6), calls=%async_computation.3 | async-start | bytes 4194304 | tf_op jit(solution)/shard_map/all_to_all | solution.py:111
  237.5 53.5 %reduce-scatter.2.cloned.1.call-start = ((), (), s32[]{:S(2)}) async-start(), calls=%async_computation.9 | async-start | bytes 1769472 | tf_op jit(solution)/shard_map/reduce_scatter | solution.py:99
Sparse Core Ops, SparseCore 0:
  10.1 32.8 all-gather.3
  48.1 28.9 all-gather.7
  106.4 28.8 all-gather.5
  241.9 36.0 reduce-scatter.1
where the time goes:
time: 299 us; the launch traced here: 298 us
  waiting for transfers between devices  166 us (56%)
  starting transfers between devices  41.8 us (14%)
  matrix products  36.1 us (12%)
  local copies, waits for them, and re-layouts  36 us (12%)
  between operations  14 us (5%)
  other arithmetic  3.43 us (1%)
    all_to_all x1, waiting for transfers between devices, local(): lax.all_to_all(slot_grads, 'expert', split_axis=0, concat_axis=0, tiled=T...  45.5 us
    all_to_all x1, waiting for transfers between devices, local(): lax.all_to_all(slot_inputs, 'expert', split_axis=0, concat_axis=0, tiled=...  44 us
    all_to_all x1, waiting for transfers between devices, local(): lax.all_to_all(out_slots, 'expert', split_axis=0, concat_axis=0, tiled=True)  34.3 us
    all_to_all x1, waiting for transfers between devices, local(): lax.all_to_all(part_slots, 'expert', split_axis=0, concat_axis=0, tiled=T...  31.6 us
    all_to_all x1, starting transfers between devices, local(): lax.all_to_all(slot_gates, 'expert', split_axis=0, concat_axis=0, tiled=T...  16.6 us
    all_to_all x1, waiting for transfers between devices, local(): lax.all_to_all(slot_gates, 'expert', split_axis=0, concat_axis=0, tiled=T...  8.75 us
    all_to_all x1, starting transfers between devices, local(): lax.all_to_all(part_slots, 'expert', split_axis=0, concat_axis=0, tiled=T...  6.81 us
    all_to_all x1, starting transfers between devices, local(): lax.all_to_all(out_slots, 'expert', split_axis=0, concat_axis=0, tiled=True)  6.77 us
  transfers between devices with their start and end apart: 9, of which 5 were waited for; matrix products, arithmetic and copies ran while one was open for 21% of the time, Pallas kernels for 0%

commit v1 on v0

v1 whole, which is shorter than its diff:
```python
import functools

import jax
import jax.numpy as jnp
from jax import lax
from jax.experimental import pallas as pl
from jax.experimental.pallas import tpu as pltpu
from jax.sharding import PartitionSpec as P

BF = jnp.bfloat16
F32 = jnp.float32
NT = (((1,), (1,)), ((), ()))
TN = (((0,), (0,)), ((), ()))


def iota(shape, axis):
    return lax.broadcasted_iota(jnp.int32, shape, axis)


def slot_keys(routes_ref, experts):
    toks = routes_ref.shape[1]
    rows = iota((experts, toks), 0)
    first = routes_ref[0:1, :] == rows
    second = routes_ref[1:2, :] == rows
    named = jnp.where(first, 1.0, jnp.where(second, 1.0, 0.0))
    earlier = jnp.where(iota((toks, toks), 0) < iota((toks, toks), 1), 1.0, 0.0).astype(BF)
    before = jnp.dot(named.astype(BF), earlier, preferred_element_type=F32)
    return jnp.where(named > 0.5, before, -1.0), first, second


def dispatch_kernel(experts, cap, routes_ref, gates_ref, tokens_ref, grads_ref, send_ref, stacked_ref, out_ref, in_sems, out_sems):
    toks, dim = tokens_ref.shape
    half = dim // 2
    rows = 4 * cap
    loads = []
    for a, ref in enumerate((tokens_ref, grads_ref)):
        for c in range(2):
            at = 2 * a + c
            loads.append(pltpu.make_async_copy(
                ref.at[:, pl.ds(c * half, half)], stacked_ref.at[pl.ds(at * toks, toks), :], in_sems.at[at]
            ))
            loads[-1].start()
    keys, first, second = slot_keys(routes_ref, experts)
    gates = gates_ref[...].astype(F32)
    gate = jnp.where(first, gates[0:1, :], jnp.where(second, gates[1:2, :], 0.0))
    block = 16
    size = block * rows
    q = iota((block, rows, toks), 1)
    slot = (q % cap).astype(F32)
    kind = (q // cap) % 2
    part = q // (2 * cap)
    for load in loads:
        load.wait()
    stores = []
    for b in range(experts // block):
        key = keys[b * block:(b + 1) * block][:, None, :]
        g = gate[b * block:(b + 1) * block][:, None, :]
        value = jnp.where(key == slot, jnp.where(kind == 1, g, 1.0), 0.0)
        pieces = []
        for a in range(2):
            for c in range(2):
                piece = jnp.where((kind == a) & (part == c), value, 0.0)
                pieces.append(piece.reshape(size, toks).astype(BF))
        placing = jnp.concatenate(pieces, axis=1)
        out_ref[b * size:(b + 1) * size, :] = jnp.dot(
            placing, stacked_ref[...], preferred_element_type=F32
        ).astype(BF)
        at = pl.ds(b * size, size)
        stores.append(pltpu.make_async_copy(out_ref.at[at, :], send_ref.at[at, :], out_sems.at[b]))
        stores[-1].start()
    for store in stores:
        store.wait()


def expert_kernel(
    cap, recv_hbm, wgu_hbm, wd_hbm, ret_hbm, hidden_ref, scaled_ref, dots_ref,
    recv_ref, wgu_ref, wd_ref, x_ref, ggu_ref, part_ref, ret_ref, in_sems, recv_sems, out_sems,
):
    total, half = recv_ref.shape
    wide = ret_ref.shape[1]
    rows = 4 * cap
    block = 16
    size = block * rows
    count = block * cap
    blocks = total // size
    hid = wd_ref.shape[0]
    loads = []
    for b in range(blocks):
        at = pl.ds(b * size, size)
        loads.append(pltpu.make_async_copy(recv_hbm.at[at, :], recv_ref.at[at, :], recv_sems.at[b]))
        loads[-1].start()
    load_down = pltpu.make_async_copy(wd_hbm, wd_ref, in_sems.at[0])
    load_wgu = pltpu.make_async_copy(wgu_hbm, wgu_ref, in_sems.at[1])
    load_down.start()
    load_wgu.start()
    out_row = iota((size, 1), 0)
    in_row = iota((size, size), 1)
    group, inner = out_row // count, out_row % count
    wanted = (inner // cap) * rows + (group % 2) * (2 * cap) + (group // 2) * cap + inner % cap
    perm = jnp.where(wanted == in_row, 1.0, 0.0).astype(BF)
    for b in range(blocks):
        loads[b].wait()
        moved = jnp.dot(perm, recv_ref[b * size:(b + 1) * size, :], preferred_element_type=F32).astype(BF)
        at = slice(b * count, (b + 1) * count)
        x_ref[at, :half] = moved[0:count]
        x_ref[at, half:] = moved[count:2 * count]
        scaled_ref[at, :half] = moved[2 * count:3 * count]
        scaled_ref[at, half:] = moved[3 * count:]
    load_down.wait()
    hidden_grad = lax.dot_general(scaled_ref[...], wd_ref[...], NT, preferred_element_type=F32)
    load_wgu.wait()
    pre_gate = jnp.dot(x_ref[...], wgu_ref[:, :hid], preferred_element_type=F32)
    pre_up = jnp.dot(x_ref[...], wgu_ref[:, hid:], preferred_element_type=F32)
    squash = jax.nn.sigmoid(pre_gate)
    activated = pre_gate * squash
    hidden = (activated * pre_up).astype(BF)
    hidden_ref[...] = hidden
    ggu_ref[:, :hid] = (hidden_grad * pre_up * squash * (1.0 + pre_gate * (1.0 - squash))).astype(BF)
    ggu_ref[:, hid:] = (hidden_grad * activated).astype(BF)
    product = hidden.astype(F32) * hidden_grad
    folded = product[:, 0:128]
    for j in range(1, hid // 128):
        folded = folded + product[:, j * 128:(j + 1) * 128]
    dots_ref[...] = jnp.sum(folded.T, axis=0, keepdims=True)
    source, inner = out_row // rows, out_row % rows
    wanted = (inner // cap) * count + source * cap + inner % cap
    perm = jnp.where(wanted == in_row, 1.0, 0.0).astype(BF)
    for c in range(4):
        piece = lax.dot_general(
            ggu_ref[...], wgu_ref[c * wide:(c + 1) * wide, :], NT, preferred_element_type=F32
        ).astype(BF)
        for b in range(blocks):
            part_ref[b * size + c * count:b * size + (c + 1) * count, :] = piece[b * count:(b + 1) * count]
    stores = []
    for b in range(blocks):
        ret_ref[b * size:(b + 1) * size, :] = jnp.dot(
            perm, part_ref[b * size:(b + 1) * size, :], preferred_element_type=F32
        ).astype(BF)
        at = pl.ds(b * size, size)
        stores.append(pltpu.make_async_copy(ret_ref.at[at, :], ret_hbm.at[at, :], out_sems.at[b]))
        stores[-1].start()
    for store in stores:
        store.wait()


def down_kernel(hidden_ref, scaled_ref, down_hbm, down_ref, sems):
    step = 512
    stores = []
    for j in range(scaled_ref.shape[1] // step):
        at = slice(j * step, (j + 1) * step)
        down_ref[:, at] = lax.dot_general(
            hidden_ref[...], scaled_ref[:, at], TN, preferred_element_type=F32
        ).astype(BF)
        cols = pl.ds(j * step, step)
        stores.append(pltpu.make_async_copy(down_ref.at[:, cols], down_hbm.at[:, cols], sems.at[j]))
        stores[-1].start()
    for store in stores:
        store.wait()


def gate_kernel(experts, cap, me_ref, routes_ref, gates_ref, dots_ref, gate_grad_ref, gather_ref):
    toks = routes_ref.shape[1]
    rows = 4 * cap
    keys, first, second = slot_keys(routes_ref, experts)
    dots = dots_ref[...]
    lane = iota(dots.shape, 1) - me_ref[0] * cap
    mine = jnp.zeros((experts, toks), F32)
    for s in range(cap):
        column = jnp.sum(jnp.where(lane == s, dots, 0.0), axis=1, keepdims=True)
        mine = mine + jnp.where(keys == float(s), column, 0.0)
    gates = gates_ref[...].astype(F32)
    one = jnp.sum(jnp.where(first, mine, 0.0), axis=0, keepdims=True) / gates[0:1, :]
    two = jnp.sum(jnp.where(second, mine, 0.0), axis=0, keepdims=True) / gates[1:2, :]
    gate_grad_ref[...] = jnp.concatenate([one, two], axis=0).astype(BF)
    q = iota((experts, rows, toks), 1)
    value = jnp.where(keys[:, None, :] == (q % cap).astype(F32), 1.0, 0.0)
    for c in range(4):
        piece = jnp.where(q // cap == c, value, 0.0).reshape(experts * rows, toks)
        gather_ref[c * toks:(c + 1) * toks, :] = piece.T.astype(BF)


def combine_kernel(gather_ref, back_ref, token_grad_ref):
    toks = token_grad_ref.shape[0]
    wide = back_ref.shape[1]
    for c in range(4):
        token_grad_ref[:, c * wide:(c + 1) * wide] = jnp.dot(
            gather_ref[c * toks:(c + 1) * toks, :], back_ref[...], preferred_element_type=F32
        ).astype(BF)


VMEM = pl.BlockSpec(memory_space=pltpu.VMEM)
SMEM = pl.BlockSpec(memory_space=pltpu.SMEM)
HBM = pl.BlockSpec(memory_space=pltpu.HBM)


def call(kernel, ins, outs, scratch=(), limit=16, flops=0, moved=0):
    return pl.pallas_call(
        kernel,
        out_shape=tuple(jax.ShapeDtypeStruct(shape, kind) for shape, kind, _ in outs),
        in_specs=list(ins),
        out_specs=tuple(spec for _, _, spec in outs),
        scratch_shapes=list(scratch),
        compiler_params=pltpu.CompilerParams(vmem_limit_bytes=limit * 1024 * 1024),
        cost_estimate=pl.CostEstimate(flops=flops, bytes_accessed=moved, transcendentals=0),
    )


def local(tokens, routes, route_gates, out_grad, w_gate, w_up, w_down):
    experts = w_gate.shape[0] * lax.axis_size("expert")
    toks, fan_out = routes.shape
    dim = tokens.shape[1]
    hid = w_gate.shape[2]
    cap = 3 * toks * fan_out // (2 * experts)
    slots = experts * cap
    routes_t = routes.T
    gates_t = route_gates.T
    wd_full = lax.all_gather(w_down[0], "dp", axis=0, tiled=True)
    wgu = lax.all_gather(jnp.concatenate([w_gate[0], w_up[0]], axis=1), "dp", axis=0, tiled=True)

    (send,) = call(
        functools.partial(dispatch_kernel, experts, cap),
        (VMEM, VMEM, HBM, HBM),
        [((4 * slots, dim // 2), BF, HBM)],
        [
            pltpu.VMEM((4 * toks, dim // 2), BF), pltpu.VMEM((4 * slots, dim // 2), BF),
            pltpu.SemaphoreType.DMA((4,)), pltpu.SemaphoreType.DMA((experts // 16,)),
        ],
        limit=63, flops=2 * 4 * slots * 4 * toks * dim // 2, moved=8 * slots * dim,
    )(routes_t, gates_t, tokens, out_grad)
    recv = lax.all_to_all(
        send.reshape(experts, 4 * cap, dim // 2), "expert", split_axis=0, concat_axis=0, tiled=True
    ).reshape(4 * slots, dim // 2)

    ret, hidden, scaled, dots = call(
        functools.partial(expert_kernel, cap),
        (HBM, HBM, HBM),
        [
            ((4 * slots, dim // 4), BF, HBM), ((slots, hid), BF, VMEM), ((slots, dim), BF, VMEM),
            ((1, slots), F32, VMEM),
        ],
        [
            pltpu.VMEM((4 * slots, dim // 2), BF), pltpu.VMEM((dim, 2 * hid), BF), pltpu.VMEM((hid, dim), BF), pltpu.VMEM((slots, dim), BF),
            pltpu.VMEM((slots, 2 * hid), BF), pltpu.VMEM((4 * slots, dim // 4), BF),
            pltpu.VMEM((4 * slots, dim // 4), BF),
            pltpu.SemaphoreType.DMA((2,)), pltpu.SemaphoreType.DMA((experts // 16,)),
            pltpu.SemaphoreType.DMA((experts // 16,)),
        ],
        limit=62, flops=10 * slots * dim * hid, moved=16 * slots * dim,
    )(recv, wgu, wd_full)
    dots_all = lax.all_gather(dots, "expert", axis=0, tiled=True)
    back = lax.all_to_all(
        ret.reshape(experts, 4 * cap, dim // 4), "expert", split_axis=0, concat_axis=0, tiled=True
    ).reshape(4 * slots, dim // 4)
    (down,) = call(
        down_kernel, (VMEM, VMEM),
        [((hid, dim), BF, HBM)],
        [pltpu.VMEM((hid, dim), BF), pltpu.SemaphoreType.DMA((dim // 512,))],
        flops=2 * slots * dim * hid, moved=4 * slots * dim,
    )(hidden, scaled)
    down_grad = lax.psum_scatter(down, "dp", scatter_dimension=0, tiled=True)[None]
    me = lax.axis_index("expert").astype(jnp.int32).reshape(1)
    gate_grad, gather = call(
        functools.partial(gate_kernel, experts, cap),
        (SMEM, VMEM, VMEM, VMEM),
        [((fan_out, toks), BF, VMEM), ((4 * toks, 4 * slots), BF, VMEM)],
        limit=24, flops=1000000, moved=4 * slots * dim,
    )(me, routes_t, gates_t, dots_all)
    (token_grad,) = call(
        combine_kernel, (VMEM, VMEM),
        [((toks, dim), BF, VMEM)],
        flops=2 * 4 * toks * 4 * slots * dim // 4, moved=4 * slots * dim,
    )(gather, back)
    return token_grad, gate_grad.T, down_grad


def solution(mesh):
    rows = P(("dp", "expert"), None)
    weights = P("expert", "dp", None)
    return jax.shard_map(
        local,
        mesh=mesh,
        in_specs=(rows, rows, rows, rows, weights, weights, weights),
        out_specs=(rows, rows, weights),
        check_vma=False,
    )
```

time: 299 us -> 230 us (0.77)
  waiting for transfers between devices: 166 us -> 77.6 us
  blocking collectives: 0 us -> 74.7 us
  matrix products: 36.1 us -> 0 us
  local copies, waits for them, and re-layouts: 36 us -> 0.66 us
  Pallas kernels: 0 us -> 20 us
    all_to_all x5 -> x2, waiting for transfers between devices: 164 us -> 28 us  [the longest x1 28 us: local(): lax.all_to_all(send.reshape(experts, 4 * cap, dim // 2), 'expert', split_...]
    all_gather x0 -> x1, blocking collectives: none -> 74.7 us  [local(): dots_all = lax.all_gather(dots, 'expert', axis=0, tiled=True)]
    all_gather x3 -> x2, waiting for transfers between devices: 0.02 us -> 48.9 us  [the longest x1 36.3 us: local(): lax.all_gather(jnp.concatenate([w_gate[0], w_up[0]], axis=1), 'dp', axis=...]
    dot_general x16 -> x0, matrix products: 36.1 us -> none  [the longest x2 4.2 us: input_rows(): lax.dot_general(gate_rows, gate_mat, CONTRACT_LAST, preferred_element_typ...]
    pallas_call x0 -> x5, Pallas kernels: none -> 20 us  [the longest x1 10.6 us: local(): call(functools.partial(expert_kernel, cap), (HBM, HBM, HBM), [((4 * slots...]
    reshape x7 -> x0, local copies, waits for them, and re-layouts: 15.7 us -> none  [the longest x1 3.73 us: local(): back_outputs.reshape(slot_count, model_dim)]
    another operation x5 -> x0, local copies, waits for them, and re-layouts: 10.3 us -> none  [the longest x1 3.88 us: local(): part_slots = input_part.reshape(experts, capacity, model_dim)]
    convert_element_type x3 -> x0, local copies, waits for them, and re-layouts: 5.68 us -> none  [the longest x1 3.69 us: local(): scaled = (recv_gates.reshape(slot_count, 1).astype(jnp.float32) * grads_f...]
  transfers between devices with their start and end apart: 9 -> 5, of which waited for: 5 -> 3; matrix products, arithmetic and copies ran while one was open for 21% -> 0% of each run, Pallas kernels for 0% -> 4%
where the time goes in v1:
time: 230 us; the launch traced here: 229 us
  waiting for transfers between devices  77.6 us (34%)
  blocking collectives  74.7 us (32%)
  starting transfers between devices  41.5 us (18%)
  Pallas kernels  20 us (9%)
  between operations  13.9 us (6%)
    all_gather x1, blocking collectives, local(): dots_all = lax.all_gather(dots, 'expert', axis=0, tiled=True)  74.7 us
    all_gather x1, waiting for transfers between devices, local(): lax.all_gather(jnp.concatenate([w_gate[0], w_up[0]], axis=1), 'dp', axis=...  36.3 us
    all_to_all x1, waiting for transfers between devices, local(): lax.all_to_all(send.reshape(experts, 4 * cap, dim // 2), 'expert', split_...  28 us
    all_to_all x1, starting transfers between devices, local(): lax.all_to_all(ret.reshape(experts, 4 * cap, dim // 4), 'expert', split_a...  24.4 us
    all_to_all x1, starting transfers between devices, local(): lax.all_to_all(send.reshape(experts, 4 * cap, dim // 2), 'expert', split_...  17 us
    all_gather x1, waiting for transfers between devices, local(): wd_full = lax.all_gather(w_down[0], 'dp', axis=0, tiled=True)  12.6 us
    pallas_call x1, Pallas kernels, local(): call(functools.partial(expert_kernel, cap), (HBM, HBM, HBM), [((4 * slots...  10.6 us
    pallas_call x1, Pallas kernels, local(): call(functools.partial(dispatch_kernel, experts, cap), (VMEM, VMEM, HBM,...  4.69 us
  transfers between devices with their start and end apart: 5, of which 3 were waited for; matrix products, arithmetic and copies ran while one was open for 0% of the time, Pallas kernels for 4%

profile of v1, /device:TPU:6, one launch (start us, length us, event | category | flops | bytes accessed | tf_op | source)
XLA Modules:
  0.0 229.1 jit_solution(15014428186884355117)
XLA Ops:
  7.2 0.0 all-gather.7.cloned.1.call-start
  7.2 0.7 all-gather.7.cloned.1.call-update
  7.9 4.7 %shard_map.94 = bf16[1536,1024]{1,0:T(8,128)(2,1)} custom-call(s32[2,128]{1,0:T(2,128)} %bitcast.18, bf16[2,128]{1,0:T(2,128)(2,1)} %bitcast.20, bf16[128,2048]{1,0:T(8,128)(2,1)} %tokens_ref.1, bf16[128,2048]{1,0:T(8,128)(2,1)} %grads_ref.1), custom_call_target="tpu_custom_call" | custom-call | flops 1610612736 | bytes 6291456 | tf_op jit(solution)/shard_map/pallas_call | solution.py:220
  12.6 0.0 copy-start.4
  12.6 0.0 copy-start.5
  12.6 17.0 %all-to-all-start = ((bf16[64,24,1024]{2,1,0:T(8,128)(2,1)}), bf16[64,24,1024]{2,1,0:T(8,128)(2,1)}, u32[]{:S(2)}, u32[]{:S(2)}) async-start(bf16[64,24,1024]{2,1,0:T(8,128)(2,1)} %bitcast.22), calls=%async_computation | async-start | bytes 6291456 | tf_op jit(solution)/shard_map/all_to_all | solution.py:230
  29.6 0.0 all-gather.5.cloned.1.call-start
  29.6 0.0 copy-done.4
  29.6 0.0 copy-done.5
  29.7 0.8 pad_maximum_fusion
  30.4 0.0 all-gather.5.cloned.1.call-update
  30.5 12.6 %all-gather.7.cloned.1.call-done = bf16[1,384,2048]{2,1,0:T(8,128)(2,1)} async-done(((bf16[1,48,2048]{2,1,0:T(8,128)(2,1)}), bf16[1,384,2048]{2,1,0:T(8,128)(2,1)}) %all-gather.7.cloned.1.call-update) | async-done | bytes 1572880 | tf_op jit(solution)/shard_map/all_gather | solution.py:217
  43.0 36.3 %all-gather.5.cloned.1.call-done.wgu_hbm = bf16[2048,768]{1,0:T(8,128)(2,1)} async-done(((bf16[256,768]{1,0:T(8,128)(2,1)}), bf16[2048,768]{1,0:T(8,128)(2,1)}) %all-gather.5.cloned.1.call-update) | async-done | bytes 3145744 | tf_op jit(solution)/shard_map/all_gather | solution.py:218
  79.3 28.0 %all-to-all-done = bf16[64,24,1024]{2,1,0:T(8,128)(2,1)} async-done(((bf16[64,24,1024]{2,1,0:T(8,128)(2,1)}), bf16[64,24,1024]{2,1,0:T(8,128)(2,1)}, u32[]{:S(2)}, u32[]{:S(2)}) %all-to-all-start) | async-done | bytes 3145760 | tf_op jit(solution)/shard_map/all_to_all | solution.py:230
  107.3 10.6 %shard_map.95 = (bf16[1536,512]{1,0:T(8,128)(2,1)}, bf16[384,384]{1,0:T(8,128)(2,1)}, bf16[384,2048]{1,0:T(8,128)(2,1)}, f32[1,384]{1,0:T(1,128)}) custom-call(bf16[1536,1024]{1,0:T(8,128)(2,1)} %bitcast.4.recv_hbm, bf16[2048,768]{1,0:T(8,128)(2,1)} %all-gather.5.cloned.1.call-done.wgu_hbm, bf16[384,2048]{1,0:T(8,128)(2,1)} %bitcast.27), custom_call_target="tpu_custom_call" | custom-call | flops 3019898880 | bytes 12582912 | tf_op jit(solution)/shard_map/pallas_call | solution.py:234
  118.0 0.0 copy-start
  118.0 0.0 copy-start.1
  118.0 24.4 %all-to-all-start.1 = ((bf16[64,24,512]{2,1,0:T(8,128)(2,1)}), bf16[64,24,512]{2,1,0:T(8,128)(2,1)S(1)}, u32[]{:S(2)}, u32[]{:S(2)}) async-start(bf16[64,24,512]{2,1,0:T(8,128)(2,1)} %bitcast.23), calls=%async_computation.1 | async-start | bytes 3145728 | tf_op jit(solution)/shard_map/all_to_all | solution.py:251
  142.4 0.0 reduce-scatter.2.cloned.1.call-start
  142.5 0.0 copy-done
  142.5 0.0 copy-done.1
  142.5 1.8 shard_map.98
  144.3 0.0 copy-start.6
  144.3 0.0 copy-start.2
  144.3 0.0 copy-start.3
  144.3 0.0 reduce-scatter.2.cloned.1.call-update
  144.4 0.6 copy-done.6
  145.0 74.7 %all-gather.1 = f32[64,1,384]{2,1,0:T(1,128)S(1)} all-gather(f32[1,1,384]{2,1,0:T(1,128)S(1)} %bitcast.26), channel_id=1, replica_groups=mesh['dp'=8,'expert'=64] {'expert'}, dimensions={0}, use_global_device_ids=true | all-gather | bytes 99840 | tf_op jit(solution)/shard_map/all_gather | solution.py:250
  219.7 0.0 copy-done.2
  219.7 0.0 copy-done.3
  219.7 1.1 shard_map.96
  220.8 0.0 all-to-all-done.1
  220.8 1.8 shard_map.97
  222.6 0.0 reduce-scatter.2.cloned.1.call-done
  (1 shorter events, 0.0 us)
Async XLA Ops:
  7.2 35.8 %all-gather.7.cloned.1.call-start = ((), (), s32[]{:S(2)}) async-start(), calls=%async_computation.5 | async-start | bytes 1769472 | tf_op jit(solution)/shard_map/all_gather | solution.py:217
  12.6 17.0 %copy-start.4 = (bf16[1,256,384]{2,1,0:T(8,128)(2,1)S(1)}, bf16[1,256,384]{2,1,0:T(8,128)(2,1)}, u32[]{:S(2)}) copy-start(bf16[1,256,384]{2,1,0:T(8,128)(2,1)} %param.12) | copy-start | bytes 589828
  12.6 17.0 %copy-start.5 = (bf16[1,256,384]{2,1,0:T(8,128)(2,1)S(1)}, bf16[1,256,384]{2,1,0:T(8,128)(2,1)}, u32[]{:S(2)}) copy-start(bf16[1,256,384]{2,1,0:T(8,128)(2,1)} %param.11) | copy-start | bytes 589828
  12.6 94.7 %all-to-all-start = ((bf16[64,24,1024]{2,1,0:T(8,128)(2,1)}), bf16[64,24,1024]{2,1,0:T(8,128)(2,1)}, u32[]{:S(2)}, u32[]{:S(2)}) async-start(bf16[64,24,1024]{2,1,0:T(8,128)(2,1)} %bitcast.22), calls=%async_computation | async-start | bytes 6291456 | tf_op jit(solution)/shard_map/all_to_all | solution.py:230
  29.6 49.7 %all-gather.5.cloned.1.call-start = ((), (), s32[]{:S(2)}) async-start(), calls=%async_computation.3 | async-start | bytes 3538944 | tf_op jit(solution)/shard_map/all_gather | solution.py:218
  118.0 24.5 %copy-start = (bf16[384,2048]{1,0:T(8,128)(2,1)S(1)}, bf16[384,2048]{1,0:T(8,128)(2,1)}, u32[]{:S(2)}) copy-start(bf16[384,2048]{1,0:T(8,128)(2,1)} %get-tuple-element.14.scaled_ref) | copy-start | bytes 4718596
  118.0 24.5 %copy-start.1 = (bf16[384,384]{1,0:T(8,128)(2,1)S(1)}, bf16[384,384]{1,0:T(8,128)(2,1)}, u32[]{:S(2)}) copy-start(bf16[384,384]{1,0:T(8,128)(2,1)} %get-tuple-element.13.hidden_ref) | copy-start | bytes 884740
  118.0 102.8 %all-to-all-start.1 = ((bf16[64,24,512]{2,1,0:T(8,128)(2,1)}), bf16[64,24,512]{2,1,0:T(8,128)(2,1)S(1)}, u32[]{:S(2)}, u32[]{:S(2)}) async-start(bf16[64,24,512]{2,1,0:T(8,128)(2,1)} %bitcast.23), calls=%async_computation.1 | async-start | bytes 3145728 | tf_op jit(solution)/shard_map/all_to_all | solution.py:251
  142.4 80.2 %reduce-scatter.2.cloned.1.call-start = ((), (), s32[]{:S(2)}) async-start(), calls=%async_computation.4 | async-start | bytes 1769472 | tf_op jit(solution)/shard_map/reduce_scatter | solution.py:260
  144.3 0.7 copy-start.6
  144.3 75.4 %copy-start.2 = (s32[128,2]{0,1:T(2,128)S(1)}, s32[128,2]{0,1:T(2,128)}, u32[]{:S(2)}) copy-start(s32[128,2]{0,1:T(2,128)} %param.8) | copy-start | bytes 3076
  144.3 75.4 %copy-start.3 = (bf16[128,2]{0,1:T(2,128)(2,1)S(1)}, bf16[128,2]{0,1:T(2,128)(2,1)}, u32[]{:S(2)}) copy-start(bf16[128,2]{0,1:T(2,128)(2,1)} %param.9) | copy-start | bytes 1540
Sparse Core Ops, SparseCore 0:
  10.1 32.8 all-gather.6
  45.7 33.5 all-gather.4
  146.7 36.1 reduce-scatter.1

commit v2 on v1

v2 whole, which is shorter than its diff:
```python
import functools

import jax
import jax.numpy as jnp
from jax import lax
from jax.experimental import pallas as pl
from jax.experimental.pallas import tpu as pltpu
from jax.sharding import PartitionSpec as P

BF = jnp.bfloat16
F32 = jnp.float32
NT = (((1,), (1,)), ((), ()))
TN = (((0,), (0,)), ((), ()))


def iota(shape, axis):
    return lax.broadcasted_iota(jnp.int32, shape, axis)


def slot_keys(routes_ref, experts):
    toks = routes_ref.shape[1]
    rows = iota((experts, toks), 0)
    first = routes_ref[0:1, :] == rows
    second = routes_ref[1:2, :] == rows
    named = jnp.where(first, 1.0, jnp.where(second, 1.0, 0.0))
    earlier = jnp.where(iota((toks, toks), 0) < iota((toks, toks), 1), 1.0, 0.0).astype(BF)
    before = jnp.dot(named.astype(BF), earlier, preferred_element_type=F32)
    return jnp.where(named > 0.5, before, -1.0), first, second


ROWS = 8
CHUNKS = 3


def tail_slot(p, q, cap):
    return (p - cap) * CHUNKS + q


def dispatch_kernel(
    experts, cap, routes_ref, gates_ref, tokens_ref, grads_ref, send_ref, tok_ref, grad_ref, out_ref, in_sems, out_sems
):
    toks, dim = tokens_ref.shape
    wide = dim // (CHUNKS + 1)
    loads = []
    for a, (src, dst) in enumerate(((tokens_ref, tok_ref), (grads_ref, grad_ref))):
        loads.append(pltpu.make_async_copy(src, dst, in_sems.at[a]))
        loads[-1].start()
    keys, first, second = slot_keys(routes_ref, experts)
    gates = gates_ref[...].astype(F32)
    gate = jnp.where(first, gates[0:1, :], jnp.where(second, gates[1:2, :], 0.0))
    block = 16
    size = block * ROWS
    p = iota((block, ROWS, toks), 1)
    main_slot = jnp.where(p < cap, p, -2).astype(F32)
    tail_slots = [jnp.where(p < cap, -2, tail_slot(p, q, cap)).astype(F32) for q in range(CHUNKS)]
    for load in loads:
        load.wait()
    stores = []
    for b in range(experts // block):
        key = keys[b * block:(b + 1) * block][:, None, :]
        g = gate[b * block:(b + 1) * block][:, None, :]
        hits = [jnp.where(key == slot, 1.0, 0.0) for slot in [main_slot] + tail_slots]
        plain = [hit.reshape(size, toks).astype(BF) for hit in hits]
        gated = [(hit * g).reshape(size, toks).astype(BF) for hit in hits]
        at = pl.ds(b * 2 * size, 2 * size)
        for q in range(CHUNKS):
            cols = slice(q * wide, (q + 1) * wide)
            both = []
            for ref, placing in ((tok_ref, plain), (grad_ref, gated)):
                lhs = jnp.concatenate([placing[0], placing[1 + q]], axis=1)
                rhs = jnp.concatenate([ref[:, cols], ref[:, CHUNKS * wide:]], axis=0)
                both.append(jnp.dot(lhs, rhs, preferred_element_type=F32).reshape(block, ROWS, wide))
            out_ref[b * 2 * size:(b + 1) * 2 * size, cols] = (
                jnp.concatenate(both, axis=1).reshape(2 * size, wide).astype(BF)
            )
        stores.append(pltpu.make_async_copy(out_ref.at[at, :], send_ref.at[at, :], out_sems.at[b]))
        stores[-1].start()
    for store in stores:
        store.wait()


def expert_kernel(
    cap, recv_hbm, wgu_hbm, wd_hbm, ret_hbm, down_hbm,
    recv_ref, wgu_ref, wd_ref, x_ref, scaled_ref, ggu_ref, part_ref, ret_ref, down_ref,
    in_sems, recv_sems, out_sems, down_sems,
):
    hid, dim = wd_ref.shape
    wide = dim // (CHUNKS + 1)
    tail = CHUNKS * wide
    block = 16
    size = 2 * block * ROWS
    count = block * cap
    blocks = recv_ref.shape[0] // size
    loads = []
    for b in range(blocks):
        at = pl.ds(b * size, size)
        loads.append(pltpu.make_async_copy(recv_hbm.at[at, :], recv_ref.at[at, :], recv_sems.at[b]))
        loads[-1].start()
    load_down = pltpu.make_async_copy(wd_hbm, wd_ref, in_sems.at[0])
    load_wgu = pltpu.make_async_copy(wgu_hbm, wgu_ref, in_sems.at[1])
    load_down.start()
    load_wgu.start()
    out_row = iota((count, 1), 0)
    in_row = iota((count, size), 1)
    source, slot = out_row // cap, out_row % cap

    def unpack(a, q):
        row = slot if q is None else jnp.where(slot % CHUNKS == q, cap + slot // CHUNKS, -size)
        return jnp.where(source * (2 * ROWS) + a * ROWS + row == in_row, 1.0, 0.0).astype(BF)

    mains = [unpack(0, None), unpack(1, None)]
    perms = [jnp.concatenate(mains + [unpack(0, q), unpack(1, q)], axis=0) for q in range(CHUNKS)]
    for b in range(blocks):
        loads[b].wait()
        at = slice(b * count, (b + 1) * count)
        tails = None
        for q in range(CHUNKS):
            cols = slice(q * wide, (q + 1) * wide)
            moved = jnp.dot(perms[q], recv_ref[b * size:(b + 1) * size, cols], preferred_element_type=F32)
            x_ref[at, cols] = moved[:count].astype(BF)
            scaled_ref[at, cols] = moved[count:2 * count].astype(BF)
            tails = moved[2 * count:] if tails is None else tails + moved[2 * count:]
        x_ref[at, tail:] = tails[:count].astype(BF)
        scaled_ref[at, tail:] = tails[count:].astype(BF)
    load_down.wait()
    hidden_grad = lax.dot_general(scaled_ref[...], wd_ref[...], NT, preferred_element_type=F32)
    load_wgu.wait()
    pre_gate = jnp.dot(x_ref[...], wgu_ref[:, :hid], preferred_element_type=F32)
    pre_up = jnp.dot(x_ref[...], wgu_ref[:, hid:], preferred_element_type=F32)
    squash = jax.nn.sigmoid(pre_gate)
    activated = pre_gate * squash
    hidden = (activated * pre_up).astype(BF)
    ggu_ref[:, :hid] = (hidden_grad * pre_up * squash * (1.0 + pre_gate * (1.0 - squash))).astype(BF)
    ggu_ref[:, hid:] = (hidden_grad * activated).astype(BF)
    dots = jnp.sum(hidden.astype(F32) * hidden_grad, axis=1, keepdims=True)
    high = dots.astype(BF).astype(F32)
    lane = iota((dots.shape[0], 128), 1)
    pair = jnp.where(lane == 0, high, jnp.where(lane == 1, dots - high, 0.0)).astype(BF)
    stores = []
    for q in range(CHUNKS + 1):
        cols = pl.ds(q * wide, wide)
        at = slice(q * wide, (q + 1) * wide)
        down_ref[:, at] = lax.dot_general(hidden, scaled_ref[:, at], TN, preferred_element_type=F32).astype(BF)
        stores.append(pltpu.make_async_copy(down_ref.at[:, cols], down_hbm.at[:, cols], down_sems.at[q]))
        stores[-1].start()
    for q in range(CHUNKS + 1):
        at = slice(q * wide, (q + 1) * wide)
        part_ref[:, at] = lax.dot_general(
            ggu_ref[...], wgu_ref[at, :], NT, preferred_element_type=F32
        ).astype(BF)
    size = block * ROWS
    out_row = iota((size, 1), 0)
    in_row = iota((size, count), 1)
    source, p = out_row // ROWS, out_row % ROWS

    def pack(q):
        slot = jnp.where(p < cap, p, -count) if q is None else jnp.where(p < cap, -count, tail_slot(p, q, cap))
        return jnp.where(source * cap + slot == in_row, 1.0, 0.0).astype(BF)

    main = pack(None)
    perms = [jnp.concatenate([main, pack(q)], axis=1) for q in range(CHUNKS)]
    for b in range(blocks):
        at = slice(b * count, (b + 1) * count)
        out = slice(b * size, (b + 1) * size)
        for q in range(CHUNKS):
            cols = slice(q * wide, (q + 1) * wide)
            rhs = jnp.concatenate([part_ref[at, cols], part_ref[at, tail:]], axis=0)
            ret_ref[out, cols] = jnp.dot(perms[q], rhs, preferred_element_type=F32).astype(BF)
        ret_ref[out, tail:] = jnp.dot(main, pair[at], preferred_element_type=F32).astype(BF)
        rows = pl.ds(b * size, size)
        stores.append(pltpu.make_async_copy(ret_ref.at[rows, :], ret_hbm.at[rows, :], out_sems.at[b]))
        stores[-1].start()
    for store in stores:
        store.wait()


def gather_kernel(experts, cap, routes_ref, after_ref, gather_ref):
    toks = routes_ref.shape[1]
    keys, first, second = slot_keys(routes_ref, experts)
    p = iota((experts, ROWS, toks), 1)
    main_slot = jnp.where(p < cap, p, -2).astype(F32)
    slots = [main_slot] + [jnp.where(p < cap, -2, tail_slot(p, q, cap)).astype(F32) for q in range(CHUNKS)]
    pieces = [(keys, slot) for slot in slots]
    pieces += [(jnp.where(choice, keys, -1.0), main_slot) for choice in (first, second)]
    for i, (key, slot) in enumerate(pieces):
        piece = jnp.where(key[:, None, :] == slot, 1.0, 0.0).reshape(experts * ROWS, toks)
        gather_ref[i * toks:(i + 1) * toks, :] = piece.T.astype(BF)


def combine_kernel(gates_ref, gather_ref, back_ref, token_grad_ref, gate_grad_ref):
    toks, dim = token_grad_ref.shape
    wide = dim // (CHUNKS + 1)
    tail = CHUNKS * wide
    tails = None
    for q in range(CHUNKS):
        cols = slice(q * wide, (q + 1) * wide)
        lhs = jnp.concatenate([gather_ref[:toks, :], gather_ref[(1 + q) * toks:(2 + q) * toks, :]], axis=0)
        moved = jnp.dot(lhs, back_ref[:, cols], preferred_element_type=F32)
        token_grad_ref[:, cols] = moved[:toks].astype(BF)
        tails = moved[toks:] if tails is None else tails + moved[toks:]
    token_grad_ref[:, tail:] = tails.astype(BF)
    dots = jnp.dot(gather_ref[(1 + CHUNKS) * toks:, :], back_ref[:, tail:], preferred_element_type=F32)
    gates = gates_ref[...].astype(F32)
    rows = []
    for k in range(2):
        pair = dots[k * toks:(k + 1) * toks].T
        rows.append((pair[0:1] + pair[1:2]) / gates[k:k + 1])
    gate_grad_ref[...] = jnp.concatenate(rows, axis=0).astype(BF)


VMEM = pl.BlockSpec(memory_space=pltpu.VMEM)
SMEM = pl.BlockSpec(memory_space=pltpu.SMEM)
HBM = pl.BlockSpec(memory_space=pltpu.HBM)


def call(kernel, ins, outs, scratch=(), limit=16, flops=0, moved=0):
    return pl.pallas_call(
        kernel,
        out_shape=tuple(jax.ShapeDtypeStruct(shape, kind) for shape, kind, _ in outs),
        in_specs=list(ins),
        out_specs=tuple(spec for _, _, spec in outs),
        scratch_shapes=list(scratch),
        compiler_params=pltpu.CompilerParams(vmem_limit_bytes=limit * 1024 * 1024),
        cost_estimate=pl.CostEstimate(flops=flops, bytes_accessed=moved, transcendentals=0),
    )


def local(tokens, routes, route_gates, out_grad, w_gate, w_up, w_down):
    experts = w_gate.shape[0] * lax.axis_size("expert")
    toks, fan_out = routes.shape
    dim = tokens.shape[1]
    hid = w_gate.shape[2]
    cap = 3 * toks * fan_out // (2 * experts)
    slots = experts * cap
    main = CHUNKS * dim // (CHUNKS + 1)
    packed = experts * ROWS
    DMA = pltpu.SemaphoreType.DMA
    routes_t = routes.T
    gates_t = route_gates.T
    wd_full = lax.all_gather(w_down[0], "dp", axis=0, tiled=True)
    wgu = lax.all_gather(jnp.concatenate([w_gate[0], w_up[0]], axis=1), "dp", axis=0, tiled=True)

    (send,) = call(
        functools.partial(dispatch_kernel, experts, cap),
        (VMEM, VMEM, HBM, HBM),
        [((2 * packed, main), BF, HBM)],
        [
            pltpu.VMEM((toks, dim), BF), pltpu.VMEM((toks, dim), BF), pltpu.VMEM((2 * packed, main), BF),
            DMA((2,)), DMA((experts // 16,)),
        ],
        limit=63, flops=8 * packed * toks * main, moved=4 * packed * main,
    )(routes_t, gates_t, tokens, out_grad)
    recv = lax.all_to_all(
        send.reshape(experts, 2 * ROWS, main), "expert", split_axis=0, concat_axis=0, tiled=True
    ).reshape(2 * packed, main)

    ret, down = call(
        functools.partial(expert_kernel, cap),
        (HBM, HBM, HBM),
        [((packed, main + 128), BF, HBM), ((hid, dim), BF, HBM)],
        [
            pltpu.VMEM((2 * packed, main), BF), pltpu.VMEM((dim, 2 * hid), BF), pltpu.VMEM((hid, dim), BF),
            pltpu.VMEM((slots, dim), BF), pltpu.VMEM((slots, dim), BF), pltpu.VMEM((slots, 2 * hid), BF),
            pltpu.VMEM((slots, dim), BF), pltpu.VMEM((packed, main + 128), BF), pltpu.VMEM((hid, dim), BF),
            DMA((2,)), DMA((experts // 16,)), DMA((experts // 16,)), DMA((CHUNKS + 1,)),
        ],
        limit=62, flops=12 * slots * dim * hid, moved=16 * slots * dim,
    )(recv, wgu, wd_full)
    down_grad = lax.psum_scatter(down, "dp", scatter_dimension=0, tiled=True)[None]
    back = lax.all_to_all(
        ret.reshape(experts, ROWS, main + 128), "expert", split_axis=0, concat_axis=0, tiled=True
    ).reshape(packed, main + 128)
    (gather,) = call(
        functools.partial(gather_kernel, experts, cap),
        (VMEM, HBM),
        [(((3 + CHUNKS) * toks, packed), BF, VMEM)],
        limit=62, flops=1000000, moved=12 * toks * packed,
    )(routes_t, wd_full)
    token_grad, gate_grad = call(
        combine_kernel, (VMEM, VMEM, VMEM),
        [((toks, dim), BF, VMEM), ((fan_out, toks), BF, VMEM)],
        flops=4 * toks * packed * dim, moved=4 * packed * dim,
    )(gates_t, gather, back)
    return token_grad, gate_grad.T, down_grad


def solution(mesh):
    rows = P(("dp", "expert"), None)
    weights = P("expert", "dp", None)
    return jax.shard_map(
        local,
        mesh=mesh,
        in_specs=(rows, rows, rows, rows, weights, weights, weights),
        out_specs=(rows, rows, weights),
        check_vma=False,
    )
```

time: 230 us -> 193 us (0.84)
  blocking collectives: 74.7 us -> 0 us
  waiting for transfers between devices: 77.6 us -> 118 us
  Pallas kernels: 20 us -> 17.1 us
    all_gather x1 -> x0, blocking collectives: 74.7 us -> none  [local(): dots_all = lax.all_gather(dots, 'expert', axis=0, tiled=True)]
    all_to_all x2, waiting for transfers between devices: 28 us -> 67.5 us  [the longest x1 40.1 us: local(): lax.all_to_all(ret.reshape(experts, ROWS, main + 128), 'expert', split_ax...]
    pallas_call x4 -> x3, Pallas kernels: 15.3 us -> 13.1 us  [the longest x1 9.65 us: local(): call(functools.partial(expert_kernel, cap), (HBM, HBM, HBM), [((packed, m...]
  transfers between devices with their start and end apart: 5 -> 5, of which waited for: 3 -> 4; matrix products, arithmetic and copies ran while one was open for 0% -> 0% of each run, Pallas kernels for 4% -> 4%
where the time goes in v2:
time: 193 us; the launch traced here: 192 us
  waiting for transfers between devices  118 us (61%)
  starting transfers between devices  41.1 us (21%)
  Pallas kernels  17.1 us (9%)
  between operations  13.8 us (7%)
    all_to_all x1, waiting for transfers between devices, local(): lax.all_to_all(ret.reshape(experts, ROWS, main + 128), 'expert', split_ax...  40.1 us
    all_gather x1, waiting for transfers between devices, local(): lax.all_gather(jnp.concatenate([w_gate[0], w_up[0]], axis=1), 'dp', axis=...  36.3 us
    all_to_all x1, waiting for transfers between devices, local(): lax.all_to_all(send.reshape(experts, 2 * ROWS, main), 'expert', split_axi...  27.5 us
    all_to_all x1, starting transfers between devices, local(): lax.all_to_all(ret.reshape(experts, ROWS, main + 128), 'expert', split_ax...  24 us
    all_to_all x1, starting transfers between devices, local(): lax.all_to_all(send.reshape(experts, 2 * ROWS, main), 'expert', split_axi...  17 us
    all_gather x1, waiting for transfers between devices, local(): wd_full = lax.all_gather(w_down[0], 'dp', axis=0, tiled=True)  13.3 us
    pallas_call x1, Pallas kernels, local(): call(functools.partial(expert_kernel, cap), (HBM, HBM, HBM), [((packed, m...  9.65 us
    pallas_call x1, Pallas kernels, local(): call(functools.partial(dispatch_kernel, experts, cap), (VMEM, VMEM, HBM,...  3.97 us
  transfers between devices with their start and end apart: 5, of which 4 were waited for; matrix products, arithmetic and copies ran while one was open for 0% of the time, Pallas kernels for 4%

profile of v2, /device:TPU:6, one launch (start us, length us, event | category | flops | bytes accessed | tf_op | source)
XLA Modules:
  0.0 192.4 jit_solution(7055160765452447683)
XLA Ops:
  7.2 0.0 all-gather.6.cloned.1.call-start
  7.2 0.7 all-gather.6.cloned.1.call-update
  7.9 4.0 %shard_map.95 = bf16[1024,1536]{1,0:T(8,128)(2,1)} custom-call(s32[2,128]{1,0:T(2,128)} %bitcast.20, bf16[2,128]{1,0:T(2,128)(2,1)} %bitcast.12, bf16[128,2048]{1,0:T(8,128)(2,1)} %tokens_ref.1, bf16[128,2048]{1,0:T(8,128)(2,1)} %grads_ref.1), custom_call_target="tpu_custom_call" | custom-call | flops 805306368 | bytes 3145728 | tf_op jit(solution)/shard_map/pallas_call | solution.py:243
  11.9 0.0 copy-start.2
  11.9 0.0 copy-start.3
  11.9 17.0 %all-to-all-start = ((bf16[64,16,1536]{2,1,0:T(8,128)(2,1)}), bf16[64,16,1536]{2,1,0:T(8,128)(2,1)}, u32[]{:S(2)}, u32[]{:S(2)}) async-start(bf16[64,16,1536]{2,1,0:T(8,128)(2,1)} %bitcast.14), calls=%async_computation | async-start | bytes 6291456 | tf_op jit(solution)/shard_map/all_to_all | solution.py:253
  28.9 0.0 all-gather.4.cloned.1.call-start
  28.9 0.0 copy-done.2
  28.9 0.0 copy-done.3
  28.9 0.8 pad_maximum_fusion
  29.7 0.0 all-gather.4.cloned.1.call-update
  29.7 13.3 %all-gather.6.cloned.1.call-done = bf16[1,384,2048]{2,1,0:T(8,128)(2,1)} async-done(((bf16[1,48,2048]{2,1,0:T(8,128)(2,1)}), bf16[1,384,2048]{2,1,0:T(8,128)(2,1)}) %all-gather.6.cloned.1.call-update) | async-done | bytes 1572880 | tf_op jit(solution)/shard_map/all_gather | solution.py:240
  43.0 36.3 %all-gather.4.cloned.1.call-done.wgu_hbm = bf16[2048,768]{1,0:T(8,128)(2,1)} async-done(((bf16[256,768]{1,0:T(8,128)(2,1)}), bf16[2048,768]{1,0:T(8,128)(2,1)}) %all-gather.4.cloned.1.call-update) | async-done | bytes 3145744 | tf_op jit(solution)/shard_map/all_gather | solution.py:241
  79.3 27.5 %all-to-all-done = bf16[64,16,1536]{2,1,0:T(8,128)(2,1)} async-done(((bf16[64,16,1536]{2,1,0:T(8,128)(2,1)}), bf16[64,16,1536]{2,1,0:T(8,128)(2,1)}, u32[]{:S(2)}, u32[]{:S(2)}) %all-to-all-start) | async-done | bytes 3145760 | tf_op jit(solution)/shard_map/all_to_all | solution.py:253
  106.8 9.7 %shard_map.96 = (bf16[512,1664]{1,0:T(8,128)(2,1)}, bf16[384,2048]{1,0:T(8,128)(2,1)}) custom-call(bf16[1024,1536]{1,0:T(8,128)(2,1)} %bitcast.4.recv_hbm, bf16[2048,768]{1,0:T(8,128)(2,1)} %all-gather.4.cloned.1.call-done.wgu_hbm, bf16[384,2048]{1,0:T(8,128)(2,1)} %bitcast.16), custom_call_target="tpu_custom_call" | custom-call | flops 3623878656 | bytes 12582912 | tf_op jit(solution)/shard_map/pallas_call | solution.py:257
  116.4 24.0 %all-to-all-start.1 = ((bf16[64,8,1664]{2,1,0:T(8,128)(2,1)}), bf16[64,8,1664]{2,1,0:T(8,128)(2,1)S(1)}, u32[]{:S(2)}, u32[]{:S(2)}) async-start(bf16[64,8,1664]{2,1,0:T(8,128)(2,1)} %bitcast.15), calls=%async_computation.1 | async-start | bytes 3407872 | tf_op jit(solution)/shard_map/all_to_all | solution.py:270
  140.4 0.0 reduce-scatter.2.cloned.1.call-start
  140.5 0.0 copy-start.1
  140.5 0.7 reduce-scatter.2.cloned.1.call-update
  141.2 2.1 %shard_map.94.gather_ref = bf16[768,512]{1,0:T(8,128)(2,1)} custom-call(s32[2,128]{1,0:T(2,128)} %bitcast.21, bf16[384,2048]{1,0:T(8,128)(2,1)} %bitcast.17), custom_call_target="tpu_custom_call" | custom-call | flops 1000000 | bytes 786432 | tf_op jit(solution)/shard_map/pallas_call | solution.py:273
  143.2 40.1 %all-to-all-done.1 = bf16[64,8,1664]{2,1,0:T(8,128)(2,1)S(1)} async-done(((bf16[64,8,1664]{2,1,0:T(8,128)(2,1)}), bf16[64,8,1664]{2,1,0:T(8,128)(2,1)S(1)}, u32[]{:S(2)}, u32[]{:S(2)}) %all-to-all-start.1) | async-done | bytes 1703968 | tf_op jit(solution)/shard_map/all_to_all | solution.py:270
  183.3 0.0 copy-done.1
  183.3 0.0 copy-start
  183.3 1.1 copy-done
  184.5 1.4 shard_map.97
  185.8 0.0 reduce-scatter.2.cloned.1.call-done
Async XLA Ops:
  7.2 35.9 %all-gather.6.cloned.1.call-start = ((), (), s32[]{:S(2)}) async-start(), calls=%async_computation.5 | async-start | bytes 1769472 | tf_op jit(solution)/shard_map/all_gather | solution.py:240
  11.9 17.0 %copy-start.2 = (bf16[1,256,384]{2,1,0:T(8,128)(2,1)S(1)}, bf16[1,256,384]{2,1,0:T(8,128)(2,1)}, u32[]{:S(2)}) copy-start(bf16[1,256,384]{2,1,0:T(8,128)(2,1)} %param.12) | copy-start | bytes 589828
  11.9 17.0 %copy-start.3 = (bf16[1,256,384]{2,1,0:T(8,128)(2,1)S(1)}, bf16[1,256,384]{2,1,0:T(8,128)(2,1)}, u32[]{:S(2)}) copy-start(bf16[1,256,384]{2,1,0:T(8,128)(2,1)} %param.11) | copy-start | bytes 589828
  11.9 94.9 %all-to-all-start = ((bf16[64,16,1536]{2,1,0:T(8,128)(2,1)}), bf16[64,16,1536]{2,1,0:T(8,128)(2,1)}, u32[]{:S(2)}, u32[]{:S(2)}) async-start(bf16[64,16,1536]{2,1,0:T(8,128)(2,1)} %bitcast.14), calls=%async_computation | async-start | bytes 6291456 | tf_op jit(solution)/shard_map/all_to_all | solution.py:253
  28.9 50.4 %all-gather.4.cloned.1.call-start = ((), (), s32[]{:S(2)}) async-start(), calls=%async_computation.3 | async-start | bytes 3538944 | tf_op jit(solution)/shard_map/all_gather | solution.py:241
  116.4 66.9 %all-to-all-start.1 = ((bf16[64,8,1664]{2,1,0:T(8,128)(2,1)}), bf16[64,8,1664]{2,1,0:T(8,128)(2,1)S(1)}, u32[]{:S(2)}, u32[]{:S(2)}) async-start(bf16[64,8,1664]{2,1,0:T(8,128)(2,1)} %bitcast.15), calls=%async_computation.1 | async-start | bytes 3407872 | tf_op jit(solution)/shard_map/all_to_all | solution.py:270
  140.4 45.4 %reduce-scatter.2.cloned.1.call-start = ((), (), s32[]{:S(2)}) async-start(), calls=%async_computation.4 | async-start | bytes 1769472 | tf_op jit(solution)/shard_map/reduce_scatter | solution.py:269
  140.5 42.8 %copy-start.1 = (bf16[128,2]{0,1:T(2,128)(2,1)S(1)}, bf16[128,2]{0,1:T(2,128)(2,1)}, u32[]{:S(2)}) copy-start(bf16[128,2]{0,1:T(2,128)(2,1)} %param.9) | copy-start | bytes 1540
  183.3 1.1 copy-start
Sparse Core Ops, SparseCore 0:
  10.1 32.8 all-gather.5
  45.7 33.5 all-gather.3
  144.7 36.1 reduce-scatter.1

commit v3 on v2

--- a/solution.py
+++ b/solution.py
@@ -80,7 +80,7 @@
 
 
 def expert_kernel(
-    cap, recv_hbm, wgu_hbm, wd_hbm, ret_hbm, down_hbm,
+    cap, recv_hbm, wgu_hbm, ret_hbm, down_hbm,
     recv_ref, wgu_ref, wd_ref, x_ref, scaled_ref, ggu_ref, part_ref, ret_ref, down_ref,
     in_sems, recv_sems, out_sems, down_sems,
 ):
@@ -96,9 +96,7 @@
         at = pl.ds(b * size, size)
         loads.append(pltpu.make_async_copy(recv_hbm.at[at, :], recv_ref.at[at, :], recv_sems.at[b]))
         loads[-1].start()
-    load_down = pltpu.make_async_copy(wd_hbm, wd_ref, in_sems.at[0])
-    load_wgu = pltpu.make_async_copy(wgu_hbm, wgu_ref, in_sems.at[1])
-    load_down.start()
+    load_wgu = pltpu.make_async_copy(wgu_hbm, wgu_ref, in_sems.at[0])
     load_wgu.start()
     out_row = iota((count, 1), 0)
     in_row = iota((count, size), 1)
@@ -122,11 +120,11 @@
             tails = moved[2 * count:] if tails is None else tails + moved[2 * count:]
         x_ref[at, tail:] = tails[:count].astype(BF)
         scaled_ref[at, tail:] = tails[count:].astype(BF)
-    load_down.wait()
+    load_wgu.wait()
+    unpack_down(wgu_ref, wd_ref)
     hidden_grad = lax.dot_general(scaled_ref[...], wd_ref[...], NT, preferred_element_type=F32)
-    load_wgu.wait()
     pre_gate = jnp.dot(x_ref[...], wgu_ref[:, :hid], preferred_element_type=F32)
-    pre_up = jnp.dot(x_ref[...], wgu_ref[:, hid:], preferred_element_type=F32)
+    pre_up = jnp.dot(x_ref[...], wgu_ref[:, hid:2 * hid], preferred_element_type=F32)
     squash = jax.nn.sigmoid(pre_gate)
     activated = pre_gate * squash
     hidden = (activated * pre_up).astype(BF)
@@ -146,7 +144,7 @@
     for q in range(CHUNKS + 1):
         at = slice(q * wide, (q + 1) * wide)
         part_ref[:, at] = lax.dot_general(
-            ggu_ref[...], wgu_ref[at, :], NT, preferred_element_type=F32
+            ggu_ref[...], wgu_ref[at, :2 * hid], NT, preferred_element_type=F32
         ).astype(BF)
     size = block * ROWS
     out_row = iota((size, 1), 0)
@@ -172,6 +170,30 @@
         stores[-1].start()
     for store in stores:
         store.wait()
+
+
+def pack_kernel(gate_ref, up_ref, down_ref, out_ref):
+    hid = gate_ref.shape[1]
+    out_ref[:, :hid] = gate_ref[...]
+    out_ref[:, hid:2 * hid] = up_ref[...]
+    for r in range(down_ref.shape[0] // 16):
+        for l in range(down_ref.shape[1] // 128):
+            out_ref[l * 16:(l + 1) * 16, 2 * hid + r * 128:2 * hid + (r + 1) * 128] = (
+                down_ref[r * 16:(r + 1) * 16, l * 128:(l + 1) * 128]
+            )
+
+
+def unpack_down(packed_ref, down_ref):
+    hid, dim = down_ref.shape
+    lanes = packed_ref.shape[1] - hid
+    high = 16 * (dim // 128)
+    each = hid * high // packed_ref.shape[0]
+    for part in range(packed_ref.shape[0] // high):
+        for r in range(each // 16):
+            for l in range(dim // 128):
+                down_ref[part * each + r * 16:part * each + (r + 1) * 16, l * 128:(l + 1) * 128] = packed_ref[
+                    part * high + l * 16:part * high + (l + 1) * 16, lanes + r * 128:lanes + (r + 1) * 128
+                ]
 
 
 def gather_kernel(experts, cap, routes_ref, after_ref, gather_ref):
@@ -237,8 +259,10 @@
     DMA = pltpu.SemaphoreType.DMA
     routes_t = routes.T
     gates_t = route_gates.T
-    wd_full = lax.all_gather(w_down[0], "dp", axis=0, tiled=True)
-    wgu = lax.all_gather(jnp.concatenate([w_gate[0], w_up[0]], axis=1), "dp", axis=0, tiled=True)
+    (mine,) = call(pack_kernel, (VMEM, VMEM, VMEM), [((dim // lax.axis_size("dp"), 3 * hid), BF, VMEM)])(
+        w_gate[0], w_up[0], w_down[0]
+    )
+    weights = lax.all_gather(mine, "dp", axis=0, tiled=True)
 
     (send,) = call(
         functools.partial(dispatch_kernel, experts, cap),
@@ -256,16 +280,16 @@
 
     ret, down = call(
         functools.partial(expert_kernel, cap),
-        (HBM, HBM, HBM),
+        (HBM, HBM),
         [((packed, main + 128), BF, HBM), ((hid, dim), BF, HBM)],
         [
-            pltpu.VMEM((2 * packed, main), BF), pltpu.VMEM((dim, 2 * hid), BF), pltpu.VMEM((hid, dim), BF),
+            pltpu.VMEM((2 * packed, main), BF), pltpu.VMEM((dim, 3 * hid), BF), pltpu.VMEM((hid, dim), BF),
             pltpu.VMEM((slots, dim), BF), pltpu.VMEM((slots, dim), BF), pltpu.VMEM((slots, 2 * hid), BF),
             pltpu.VMEM((slots, dim), BF), pltpu.VMEM((packed, main + 128), BF), pltpu.VMEM((hid, dim), BF),
-            DMA((2,)), DMA((experts // 16,)), DMA((experts // 16,)), DMA((CHUNKS + 1,)),
+            DMA((1,)), DMA((experts // 16,)), DMA((experts // 16,)), DMA((CHUNKS + 1,)),
         ],
         limit=62, flops=12 * slots * dim * hid, moved=16 * slots * dim,
-    )(recv, wgu, wd_full)
+    )(recv, weights)
     down_grad = lax.psum_scatter(down, "dp", scatter_dimension=0, tiled=True)[None]
     back = lax.all_to_all(
         ret.reshape(experts, ROWS, main + 128), "expert", split_axis=0, concat_axis=0, tiled=True
@@ -275,7 +299,7 @@
         (VMEM, HBM),
         [(((3 + CHUNKS) * toks, packed), BF, VMEM)],
         limit=62, flops=1000000, moved=12 * toks * packed,
-    )(routes_t, wd_full)
+    )(routes_t, weights)
     token_grad, gate_grad = call(
         combine_kernel, (VMEM, VMEM, VMEM),
         [((toks, dim), BF, VMEM), ((fan_out, toks), BF, VMEM)],

time: 193 us -> 178 us (0.922)
  blocking collectives: 0 us -> 91.4 us
  waiting for transfers between devices: 118 us -> 39 us
  starting transfers between devices: 41.1 us -> 11 us
  local copies, waits for them, and re-layouts: 1.15 us -> 3.91 us
    all_to_all x0 -> x1, blocking collectives: none -> 91.4 us  [local(): lax.all_to_all(send.reshape(experts, 2 * ROWS, main), 'expert', split_axi...]
    all_gather x2 -> x1, waiting for transfers between devices: 49.6 us -> 0.01 us  [local(): weights = lax.all_gather(mine, 'dp', axis=0, tiled=True)]
    all_to_all x1 -> x0, waiting for transfers between devices: 27.5 us -> none  [local(): lax.all_to_all(send.reshape(experts, 2 * ROWS, main), 'expert', split_axi...]
    all_to_all x1 -> x0, starting transfers between devices: 17 us -> none  [local(): lax.all_to_all(send.reshape(experts, 2 * ROWS, main), 'expert', split_axi...]
    all_to_all x1, starting transfers between devices: 24 us -> 10.9 us  [local(): lax.all_to_all(ret.reshape(experts, ROWS, main + 128), 'expert', split_ax...]
    unnamed x8 -> x10, local copies, waits for them, and re-layouts: 1.15 us -> 3.91 us
    pallas_call x1 -> x2, Pallas kernels: 9.65 us -> 10.8 us  [the longest x1 9.93 us: local(): call(functools.partial(expert_kernel, cap), (HBM, HBM), [((packed, main +...]
  transfers between devices with their start and end apart: 5 -> 3, of which waited for: 4 -> 1; matrix products, arithmetic and copies ran while one was open for 0% -> 0% of each run, Pallas kernels for 4% -> 4%
where the time goes in v3:
time: 178 us
  blocking collectives  91.4 us (51%)
  waiting for transfers between devices  39 us (22%)
  Pallas kernels  18.3 us (10%)
  between operations  14.1 us (8%)
  starting transfers between devices  11 us (6%)
  local copies, waits for them, and re-layouts  3.91 us (2%)
    all_to_all x1, blocking collectives, local(): lax.all_to_all(send.reshape(experts, 2 * ROWS, main), 'expert', split_axi...  91.4 us
    all_to_all x1, waiting for transfers between devices, local(): lax.all_to_all(ret.reshape(experts, ROWS, main + 128), 'expert', split_ax...  38.2 us
    all_to_all x1, starting transfers between devices, local(): lax.all_to_all(ret.reshape(experts, ROWS, main + 128), 'expert', split_ax...  10.9 us
    pallas_call x1, Pallas kernels, local(): call(functools.partial(expert_kernel, cap), (HBM, HBM), [((packed, main +...  9.93 us
    pallas_call x1, Pallas kernels, local(): call(functools.partial(dispatch_kernel, experts, cap), (VMEM, VMEM, HBM,...  4.08 us
    unnamed x10, local copies, waits for them, and re-layouts  3.91 us
  transfers between devices with their start and end apart: 3, of which 1 were waited for; matrix products, arithmetic and copies ran while one was open for 0% of the time, Pallas kernels for 4%

profile of v3, /device:TPU:6, one launch (start us, length us, event | category | flops | bytes accessed | tf_op | source)
XLA Modules:
  0.0 177.6 jit_solution(6909273083796376957)
XLA Ops:
  7.2 0.0 all-gather.2.cloned.1.call-start
  7.2 0.0 copy-start.1
  7.2 0.9 copy-done.1
  8.1 0.0 copy-start.2
  8.1 0.9 copy-done.2
  9.1 0.0 copy-start.3
  9.1 0.9 copy-done.3
  10.0 0.9 shard_map.94
  10.9 0.0 all-gather.2.cloned.1.call-update
  10.9 4.1 %shard_map.96 = bf16[1024,1536]{1,0:T(8,128)(2,1)} custom-call(s32[2,128]{1,0:T(2,128)} %bitcast.20, bf16[2,128]{1,0:T(2,128)(2,1)} %bitcast.15, bf16[128,2048]{1,0:T(8,128)(2,1)} %tokens_ref.1, bf16[128,2048]{1,0:T(8,128)(2,1)} %grads_ref.1), custom_call_target="tpu_custom_call" | custom-call | flops 805306368 | bytes 3145728 | tf_op jit(solution)/shard_map/pallas_call | solution.py:267
  15.0 91.4 %all_to_all.10 = bf16[64,16,1536]{2,1,0:T(8,128)(2,1)} all-to-all(bf16[64,16,1536]{2,1,0:T(8,128)(2,1)} %bitcast.17), channel_id=1, replica_groups=mesh['dp'=8,'expert'=64] {'expert'}, dimensions={0} | all-to-all | bytes 6291456 | tf_op jit(solution)/shard_map/all_to_all | solution.py:277
  106.3 0.0 all-gather.2.cloned.1.call-done.after_ref.wgu_hbm
  106.3 9.9 %shard_map.97 = (bf16[512,1664]{1,0:T(8,128)(2,1)}, bf16[384,2048]{1,0:T(8,128)(2,1)}) custom-call(bf16[1024,1536]{1,0:T(8,128)(2,1)} %bitcast.18, bf16[2048,1152]{1,0:T(8,128)(2,1)} %all-gather.2.cloned.1.call-done.after_ref.wgu_hbm), custom_call_target="tpu_custom_call" | custom-call | flops 3623878656 | bytes 12582912 | tf_op jit(solution)/shard_map/pallas_call | solution.py:281
  116.3 10.9 %all-to-all-start.1 = ((bf16[64,8,1664]{2,1,0:T(8,128)(2,1)}), bf16[64,8,1664]{2,1,0:T(8,128)(2,1)S(1)}, u32[]{:S(2)}, u32[]{:S(2)}) async-start(bf16[64,8,1664]{2,1,0:T(8,128)(2,1)} %bitcast.19), calls=%async_computation.1 | async-start | bytes 3407872 | tf_op jit(solution)/shard_map/all_to_all | solution.py:294
  127.2 0.0 reduce-scatter.2.cloned.1.call-start
  127.2 0.7 reduce-scatter.2.cloned.1.call-update
  127.9 0.0 copy-start.4
  127.9 2.1 %shard_map.95.gather_ref = bf16[768,512]{1,0:T(8,128)(2,1)} custom-call(s32[2,128]{1,0:T(2,128)} %bitcast.21, bf16[2048,1152]{1,0:T(8,128)(2,1)} %all-gather.2.cloned.1.call-done.after_ref.wgu_hbm), custom_call_target="tpu_custom_call" | custom-call | flops 1000000 | bytes 786432 | tf_op jit(solution)/shard_map/pallas_call | solution.py:297
  130.0 38.2 %all-to-all-done.1 = bf16[64,8,1664]{2,1,0:T(8,128)(2,1)S(1)} async-done(((bf16[64,8,1664]{2,1,0:T(8,128)(2,1)}), bf16[64,8,1664]{2,1,0:T(8,128)(2,1)S(1)}, u32[]{:S(2)}, u32[]{:S(2)}) %all-to-all-start.1) | async-done | bytes 1703968 | tf_op jit(solution)/shard_map/all_to_all | solution.py:294
  168.3 0.0 copy-done.4
  168.3 0.0 copy-start
  168.3 1.1 copy-done
  169.4 1.4 shard_map.98
  170.8 0.0 reduce-scatter.2.cloned.1.call-done
Async XLA Ops:
  7.2 99.2 %all-gather.2.cloned.1.call-start = ((), (), s32[]{:S(2)}) async-start(), calls=%async_computation.3 | async-start | bytes 5308416 | tf_op jit(solution)/shard_map/all_gather | solution.py:265
  7.2 0.9 copy-start.1
  8.1 0.9 copy-start.2
  9.1 0.9 copy-start.3
  116.3 52.0 %all-to-all-start.1 = ((bf16[64,8,1664]{2,1,0:T(8,128)(2,1)}), bf16[64,8,1664]{2,1,0:T(8,128)(2,1)S(1)}, u32[]{:S(2)}, u32[]{:S(2)}) async-start(bf16[64,8,1664]{2,1,0:T(8,128)(2,1)} %bitcast.19), calls=%async_computation.1 | async-start | bytes 3407872 | tf_op jit(solution)/shard_map/all_to_all | solution.py:294
  127.2 43.6 %reduce-scatter.2.cloned.1.call-start = ((), (), s32[]{:S(2)}) async-start(), calls=%async_computation.4 | async-start | bytes 1769472 | tf_op jit(solution)/shard_map/reduce_scatter | solution.py:293
  127.9 40.3 %copy-start.4 = (bf16[128,2]{0,1:T(2,128)(2,1)S(1)}, bf16[128,2]{0,1:T(2,128)(2,1)}, u32[]{:S(2)}) copy-start(bf16[128,2]{0,1:T(2,128)(2,1)} %param.9) | copy-start | bytes 1540
  168.3 1.1 copy-start
Sparse Core Ops, SparseCore 0:
  11.0 42.3 all-gather.1
  131.4 36.0 reduce-scatter.1

commit v4 on v3

--- a/solution.py
+++ b/solution.py
@@ -37,10 +37,18 @@
 
 
 def dispatch_kernel(
-    experts, cap, routes_ref, gates_ref, tokens_ref, grads_ref, send_ref, tok_ref, grad_ref, out_ref, in_sems, out_sems
+    experts, cap, routes_ref, gates_ref, tokens_ref, grads_ref, gate_hbm, up_hbm, down_hbm, send_ref, weights_hbm,
+    tok_ref, grad_ref, out_ref, down_ref, pack_ref, in_sems, out_sems, weight_sems,
 ):
     toks, dim = tokens_ref.shape
     wide = dim // (CHUNKS + 1)
+    hid = gate_hbm.shape[1]
+    load_down = pltpu.make_async_copy(down_hbm, down_ref, weight_sems.at[3])
+    load_down.start()
+    load_slices = []
+    for i, src in enumerate((gate_hbm, up_hbm)):
+        load_slices.append(pltpu.make_async_copy(src, pack_ref.at[:, pl.ds(i * hid, hid)], weight_sems.at[i]))
+        load_slices[-1].start()
     loads = []
     for a, (src, dst) in enumerate(((tokens_ref, tok_ref), (grads_ref, grad_ref))):
         loads.append(pltpu.make_async_copy(src, dst, in_sems.at[a]))
@@ -53,9 +61,18 @@
     p = iota((block, ROWS, toks), 1)
     main_slot = jnp.where(p < cap, p, -2).astype(F32)
     tail_slots = [jnp.where(p < cap, -2, tail_slot(p, q, cap)).astype(F32) for q in range(CHUNKS)]
+    load_down.wait()
+    for r in range(down_ref.shape[0] // 16):
+        for l in range(dim // 128):
+            pack_ref[l * 16:(l + 1) * 16, 2 * hid + r * 128:2 * hid + (r + 1) * 128] = (
+                down_ref[r * 16:(r + 1) * 16, l * 128:(l + 1) * 128]
+            )
+    for load in load_slices:
+        load.wait()
+    stores = [pltpu.make_async_copy(pack_ref, weights_hbm, weight_sems.at[2])]
+    stores[0].start()
     for load in loads:
         load.wait()
-    stores = []
     for b in range(experts // block):
         key = keys[b * block:(b + 1) * block][:, None, :]
         g = gate[b * block:(b + 1) * block][:, None, :]
@@ -172,17 +189,6 @@
         store.wait()
 
 
-def pack_kernel(gate_ref, up_ref, down_ref, out_ref):
-    hid = gate_ref.shape[1]
-    out_ref[:, :hid] = gate_ref[...]
-    out_ref[:, hid:2 * hid] = up_ref[...]
-    for r in range(down_ref.shape[0] // 16):
-        for l in range(down_ref.shape[1] // 128):
-            out_ref[l * 16:(l + 1) * 16, 2 * hid + r * 128:2 * hid + (r + 1) * 128] = (
-                down_ref[r * 16:(r + 1) * 16, l * 128:(l + 1) * 128]
-            )
-
-
 def unpack_down(packed_ref, down_ref):
     hid, dim = down_ref.shape
     lanes = packed_ref.shape[1] - hid
@@ -196,38 +202,41 @@
                 ]
 
 
-def gather_kernel(experts, cap, routes_ref, after_ref, gather_ref):
-    toks = routes_ref.shape[1]
-    keys, first, second = slot_keys(routes_ref, experts)
-    p = iota((experts, ROWS, toks), 1)
-    main_slot = jnp.where(p < cap, p, -2).astype(F32)
-    slots = [main_slot] + [jnp.where(p < cap, -2, tail_slot(p, q, cap)).astype(F32) for q in range(CHUNKS)]
-    pieces = [(keys, slot) for slot in slots]
-    pieces += [(jnp.where(choice, keys, -1.0), main_slot) for choice in (first, second)]
-    for i, (key, slot) in enumerate(pieces):
-        piece = jnp.where(key[:, None, :] == slot, 1.0, 0.0).reshape(experts * ROWS, toks)
-        gather_ref[i * toks:(i + 1) * toks, :] = piece.T.astype(BF)
-
-
-def combine_kernel(gates_ref, gather_ref, back_ref, token_grad_ref, gate_grad_ref):
+def combine_kernel(experts, cap, routes_ref, gates_ref, back_ref, after_ref, token_grad_ref, gate_grad_ref):
     toks, dim = token_grad_ref.shape
     wide = dim // (CHUNKS + 1)
     tail = CHUNKS * wide
+    packed = experts * ROWS
+    keys, first, _ = slot_keys(routes_ref, experts)
+    spread = jnp.where(iota((experts, packed), 0) == iota((experts, packed), 1) // ROWS, 1.0, 0.0).astype(BF)
+    key = lax.dot_general(keys.astype(BF), spread, TN, preferred_element_type=F32)
+    one = lax.dot_general(jnp.where(first, 1.0, 0.0).astype(BF), spread, TN, preferred_element_type=F32)
+    p = iota((1, packed), 1) % ROWS
+    main_slot = jnp.where(p < cap, p, -2).astype(F32)
+    main = jnp.where(key == main_slot, 1.0, 0.0)
+    choices = jnp.concatenate([main * one, main * (1.0 - one)], axis=0).astype(BF)
+    lhs = []
+    for q in range(CHUNKS):
+        slot = jnp.where(p < cap, -2, tail_slot(p, q, cap)).astype(F32)
+        lhs.append(jnp.concatenate([main, jnp.where(key == slot, 1.0, 0.0)], axis=0).astype(BF))
     tails = None
     for q in range(CHUNKS):
         cols = slice(q * wide, (q + 1) * wide)
-        lhs = jnp.concatenate([gather_ref[:toks, :], gather_ref[(1 + q) * toks:(2 + q) * toks, :]], axis=0)
-        moved = jnp.dot(lhs, back_ref[:, cols], preferred_element_type=F32)
+        moved = jnp.dot(lhs[q], back_ref[:, cols], preferred_element_type=F32)
         token_grad_ref[:, cols] = moved[:toks].astype(BF)
         tails = moved[toks:] if tails is None else tails + moved[toks:]
     token_grad_ref[:, tail:] = tails.astype(BF)
-    dots = jnp.dot(gather_ref[(1 + CHUNKS) * toks:, :], back_ref[:, tail:], preferred_element_type=F32)
+    dots = jnp.dot(choices, back_ref[:, tail:], preferred_element_type=F32)
     gates = gates_ref[...].astype(F32)
     rows = []
     for k in range(2):
         pair = dots[k * toks:(k + 1) * toks].T
         rows.append((pair[0:1] + pair[1:2]) / gates[k:k + 1])
     gate_grad_ref[...] = jnp.concatenate(rows, axis=0).astype(BF)
+
+
+def after_kernel(down_ref, out_ref):
+    out_ref[...] = jnp.zeros_like(out_ref)
 
 
 VMEM = pl.BlockSpec(memory_space=pltpu.VMEM)
@@ -259,21 +268,19 @@
     DMA = pltpu.SemaphoreType.DMA
     routes_t = routes.T
     gates_t = route_gates.T
-    (mine,) = call(pack_kernel, (VMEM, VMEM, VMEM), [((dim // lax.axis_size("dp"), 3 * hid), BF, VMEM)])(
-        w_gate[0], w_up[0], w_down[0]
-    )
-    weights = lax.all_gather(mine, "dp", axis=0, tiled=True)
-
-    (send,) = call(
+    share = dim // lax.axis_size("dp")
+    send, mine = call(
         functools.partial(dispatch_kernel, experts, cap),
-        (VMEM, VMEM, HBM, HBM),
-        [((2 * packed, main), BF, HBM)],
+        (VMEM, VMEM, HBM, HBM, HBM, HBM, HBM),
+        [((2 * packed, main), BF, HBM), ((share, 3 * hid), BF, HBM)],
         [
             pltpu.VMEM((toks, dim), BF), pltpu.VMEM((toks, dim), BF), pltpu.VMEM((2 * packed, main), BF),
-            DMA((2,)), DMA((experts // 16,)),
+            pltpu.VMEM(w_down.shape[1:], BF), pltpu.VMEM((share, 3 * hid), BF),
+            DMA((2,)), DMA((experts // 16,)), DMA((4,)),
         ],
         limit=63, flops=8 * packed * toks * main, moved=4 * packed * main,
-    )(routes_t, gates_t, tokens, out_grad)
+    )(routes_t, gates_t, tokens, out_grad, w_gate[0], w_up[0], w_down[0])
+    weights = lax.all_gather(mine, "dp", axis=0, tiled=True)
     recv = lax.all_to_all(
         send.reshape(experts, 2 * ROWS, main), "expert", split_axis=0, concat_axis=0, tiled=True
     ).reshape(2 * packed, main)
@@ -294,17 +301,14 @@
     back = lax.all_to_all(
         ret.reshape(experts, ROWS, main + 128), "expert", split_axis=0, concat_axis=0, tiled=True
     ).reshape(packed, main + 128)
-    (gather,) = call(
-        functools.partial(gather_kernel, experts, cap),
-        (VMEM, HBM),
-        [(((3 + CHUNKS) * toks, packed), BF, VMEM)],
-        limit=62, flops=1000000, moved=12 * toks * packed,
-    )(routes_t, weights)
+    (after,) = call(
+        after_kernel, (HBM,), [((8, 128), F32, VMEM)], flops=10**11, moved=10**9,
+    )(down_grad[0])
     token_grad, gate_grad = call(
-        combine_kernel, (VMEM, VMEM, VMEM),
+        functools.partial(combine_kernel, experts, cap), (VMEM, VMEM, VMEM, VMEM),
         [((toks, dim), BF, VMEM), ((fan_out, toks), BF, VMEM)],
-        flops=4 * toks * packed * dim, moved=4 * packed * dim,
-    )(gates_t, gather, back)
+        limit=16, flops=4 * toks * packed * dim, moved=4 * packed * dim,
+    )(routes_t, gates_t, back, after)
     return token_grad, gate_grad.T, down_grad
 
 

time: 178 us -> 174 us (0.978)
  local copies, waits for them, and re-layouts: 3.91 us -> 0.93 us
  Pallas kernels: 18.3 us -> 16 us
    reduce_scatter x1, waiting for transfers between devices: 0.01 us -> 23.4 us  [local(): lax.psum_scatter(down, 'dp', scatter_dimension=0, tiled=True)[None]]
    all_to_all x1, waiting for transfers between devices: 38.2 us -> 16.5 us  [local(): lax.all_to_all(ret.reshape(experts, ROWS, main + 128), 'expert', split_ax...]
    unnamed x10 -> x6, local copies, waits for them, and re-layouts: 3.91 us -> 0.93 us
    pallas_call x3 -> x2, Pallas kernels: 4.32 us -> 1.72 us  [the longest x1 1.71 us: local(): call(functools.partial(combine_kernel, experts, cap), (VMEM, VMEM, VMEM,...]
  transfers between devices with their start and end apart: 3 -> 3, of which waited for: 1 -> 2; matrix products, arithmetic and copies ran while one was open for 0% -> 0% of each run, Pallas kernels for 4% -> 0%
where the time goes in v4:
time: 174 us; the launch traced here: 173 us
  blocking collectives  91.3 us (52%)
  waiting for transfers between devices  39.9 us (23%)
  Pallas kernels  16 us (9%)
  between operations  14.1 us (8%)
  starting transfers between devices  11.1 us (6%)
    all_to_all x1, blocking collectives, local(): lax.all_to_all(send.reshape(experts, 2 * ROWS, main), 'expert', split_axi...  91.3 us
    reduce_scatter x1, waiting for transfers between devices, local(): lax.psum_scatter(down, 'dp', scatter_dimension=0, tiled=True)[None]  23.4 us
    all_to_all x1, waiting for transfers between devices, local(): lax.all_to_all(ret.reshape(experts, ROWS, main + 128), 'expert', split_ax...  16.5 us
    all_to_all x1, starting transfers between devices, local(): lax.all_to_all(ret.reshape(experts, ROWS, main + 128), 'expert', split_ax...  11 us
    pallas_call x1, Pallas kernels, local(): call(functools.partial(expert_kernel, cap), (HBM, HBM), [((packed, main +...  9.92 us
    pallas_call x1, Pallas kernels, local(): call(functools.partial(dispatch_kernel, experts, cap), (VMEM, VMEM, HBM,...  4.38 us
  transfers between devices with their start and end apart: 3, of which 2 were waited for; matrix products, arithmetic and copies ran while one was open for 0% of the time, Pallas kernels for 0%

profile of v4, /device:TPU:6, one launch (start us, length us, event | category | flops | bytes accessed | tf_op | source)
XLA Modules:
  0.0 173.3 jit_solution(2549963617876671405)
XLA Ops:
  7.2 0.0 all-gather.2.cloned.1.call-start
  7.2 4.4 %shard_map.94 = (bf16[1024,1536]{1,0:T(8,128)(2,1)}, bf16[256,1152]{1,0:T(8,128)(2,1)}) custom-call(s32[2,128]{1,0:T(2,128)} %bitcast.13, bf16[2,128]{1,0:T(2,128)(2,1)} %bitcast.15, bf16[128,2048]{1,0:T(8,128)(2,1)} %tokens_ref.1, bf16[128,2048]{1,0:T(8,128)(2,1)} %grads_ref.1, bf16[256,384]{1,0:T(8,128)(2,1)} %bitcast.20, bf16[256,384]{1,0:T(8,128)(2,1)} %bitcast.21, ...), custom_call_target="tpu_custom_call" | custom-call | flops 805306368 | bytes 3145728 | tf_op jit(solution)/shard_map/pallas_call | solution.py:272
  11.6 0.0 all-gather.2.cloned.1.call-update
  11.6 0.0 reduce-scatter.2.cloned.1.call-start
  11.7 91.3 %all_to_all.10 = bf16[64,16,1536]{2,1,0:T(8,128)(2,1)} all-to-all(bf16[64,16,1536]{2,1,0:T(8,128)(2,1)} %bitcast.17), channel_id=1, replica_groups=mesh['dp'=8,'expert'=64] {'expert'}, dimensions={0} | all-to-all | bytes 6291456 | tf_op jit(solution)/shard_map/all_to_all | solution.py:284
  103.0 0.0 all-gather.2.cloned.1.call-done.wgu_hbm
  103.0 9.9 %shard_map.95 = (bf16[512,1664]{1,0:T(8,128)(2,1)}, bf16[384,2048]{1,0:T(8,128)(2,1)}) custom-call(bf16[1024,1536]{1,0:T(8,128)(2,1)} %bitcast.18, bf16[2048,1152]{1,0:T(8,128)(2,1)} %all-gather.2.cloned.1.call-done.wgu_hbm), custom_call_target="tpu_custom_call" | custom-call | flops 3623878656 | bytes 12582912 | tf_op jit(solution)/shard_map/pallas_call | solution.py:288
  112.9 0.0 reduce-scatter.2.cloned.1.call-update
  113.0 11.0 %all-to-all-start.1 = ((bf16[64,8,1664]{2,1,0:T(8,128)(2,1)}), bf16[64,8,1664]{2,1,0:T(8,128)(2,1)S(1)}, u32[]{:S(2)}, u32[]{:S(2)}) async-start(bf16[64,8,1664]{2,1,0:T(8,128)(2,1)} %bitcast.19), calls=%async_computation.1 | async-start | bytes 3407872 | tf_op jit(solution)/shard_map/all_to_all | solution.py:301
  124.0 23.4 %reduce-scatter.2.cloned.1.call-done.down_ref = bf16[48,2048]{1,0:T(8,128)(2,1)} async-done(((bf16[384,2048]{1,0:T(8,128)(2,1)}), bf16[48,2048]{1,0:T(8,128)(2,1)}) %reduce-scatter.2.cloned.1.call-update) | async-done | bytes 196624 | tf_op jit(solution)/shard_map/reduce_scatter | solution.py:300
  147.3 0.0 copy-start
  147.3 0.9 copy-done
  148.3 0.0 copy-start.1
  148.3 0.0 copy-start.2
  148.3 16.5 %all-to-all-done.1 = bf16[64,8,1664]{2,1,0:T(8,128)(2,1)S(1)} async-done(((bf16[64,8,1664]{2,1,0:T(8,128)(2,1)}), bf16[64,8,1664]{2,1,0:T(8,128)(2,1)S(1)}, u32[]{:S(2)}, u32[]{:S(2)}) %all-to-all-start.1) | async-done | bytes 1703968 | tf_op jit(solution)/shard_map/all_to_all | solution.py:301
  164.8 0.0 copy-done.1
  164.8 0.0 copy-done.2
  164.8 1.7 shard_map.97
  (1 shorter events, 0.0 us)
Async XLA Ops:
  7.2 95.9 %all-gather.2.cloned.1.call-start = ((), (), s32[]{:S(2)}) async-start(), calls=%async_computation.3 | async-start | bytes 5308416 | tf_op jit(solution)/shard_map/all_gather | solution.py:283
  11.6 135.7 %reduce-scatter.2.cloned.1.call-start = ((), (), s32[]{:S(2)}) async-start(), calls=%async_computation.4 | async-start | bytes 1769472 | tf_op jit(solution)/shard_map/reduce_scatter | solution.py:300
  113.0 51.8 %all-to-all-start.1 = ((bf16[64,8,1664]{2,1,0:T(8,128)(2,1)}), bf16[64,8,1664]{2,1,0:T(8,128)(2,1)S(1)}, u32[]{:S(2)}, u32[]{:S(2)}) async-start(bf16[64,8,1664]{2,1,0:T(8,128)(2,1)} %bitcast.19), calls=%async_computation.1 | async-start | bytes 3407872 | tf_op jit(solution)/shard_map/all_to_all | solution.py:301
  147.3 0.9 copy-start
  148.3 16.5 %copy-start.1 = (s32[128,2]{0,1:T(2,128)S(1)}, s32[128,2]{0,1:T(2,128)}, u32[]{:S(2)}) copy-start(s32[128,2]{0,1:T(2,128)} %param.8) | copy-start | bytes 3076
  148.3 16.5 %copy-start.2 = (bf16[128,2]{0,1:T(2,128)(2,1)S(1)}, bf16[128,2]{0,1:T(2,128)(2,1)}, u32[]{:S(2)}) copy-start(bf16[128,2]{0,1:T(2,128)(2,1)} %param.9) | copy-start | bytes 1540
Sparse Core Ops, SparseCore 0:
  11.7 42.3 all-gather.1
  113.1 34.2 reduce-scatter.1

commit v5 on v4

--- a/solution.py
+++ b/solution.py
@@ -113,33 +113,40 @@
         at = pl.ds(b * size, size)
         loads.append(pltpu.make_async_copy(recv_hbm.at[at, :], recv_ref.at[at, :], recv_sems.at[b]))
         loads[-1].start()
-    load_wgu = pltpu.make_async_copy(wgu_hbm, wgu_ref, in_sems.at[0])
+    lanes = [pl.ds(2 * hid, hid), pl.ds(0, 2 * hid)]
+    load_down, load_wgu = (
+        pltpu.make_async_copy(wgu_hbm.at[:, at], wgu_ref.at[:, at], in_sems.at[i]) for i, at in enumerate(lanes)
+    )
+    load_down.start()
     load_wgu.start()
-    out_row = iota((count, 1), 0)
-    in_row = iota((count, size), 1)
-    source, slot = out_row // cap, out_row % cap
+    few = 2 * block
 
     def unpack(a, q):
-        row = slot if q is None else jnp.where(slot % CHUNKS == q, cap + slot // CHUNKS, -size)
-        return jnp.where(source * (2 * ROWS) + a * ROWS + row == in_row, 1.0, 0.0).astype(BF)
+        height = count if q is None else few
+        out_row = iota((height, 1), 0)
+        source, half = out_row % block, out_row // block % 2
+        row = half * CHUNKS + out_row // few if q is None else cap + half
+        return jnp.where(source * (2 * ROWS) + a * ROWS + row == iota((height, size), 1), 1.0, 0.0).astype(BF)
 
     mains = [unpack(0, None), unpack(1, None)]
-    perms = [jnp.concatenate(mains + [unpack(0, q), unpack(1, q)], axis=0) for q in range(CHUNKS)]
+    perm = jnp.concatenate(mains + [unpack(0, 0), unpack(1, 0)], axis=0)
     for b in range(blocks):
         loads[b].wait()
         at = slice(b * count, (b + 1) * count)
-        tails = None
         for q in range(CHUNKS):
             cols = slice(q * wide, (q + 1) * wide)
-            moved = jnp.dot(perms[q], recv_ref[b * size:(b + 1) * size, cols], preferred_element_type=F32)
-            x_ref[at, cols] = moved[:count].astype(BF)
-            scaled_ref[at, cols] = moved[count:2 * count].astype(BF)
-            tails = moved[2 * count:] if tails is None else tails + moved[2 * count:]
-        x_ref[at, tail:] = tails[:count].astype(BF)
-        scaled_ref[at, tail:] = tails[count:].astype(BF)
-    load_wgu.wait()
+            tails = slice(b * count + q * few, b * count + (q + 1) * few)
+            moved = jnp.dot(
+                perm, recv_ref[b * size:(b + 1) * size, cols], preferred_element_type=F32
+            ).astype(BF)
+            x_ref[at, cols] = moved[:count]
+            scaled_ref[at, cols] = moved[count:2 * count]
+            x_ref[tails, tail:] = moved[2 * count:2 * count + few]
+            scaled_ref[tails, tail:] = moved[2 * count + few:]
+    load_down.wait()
     unpack_down(wgu_ref, wd_ref)
     hidden_grad = lax.dot_general(scaled_ref[...], wd_ref[...], NT, preferred_element_type=F32)
+    load_wgu.wait()
     pre_gate = jnp.dot(x_ref[...], wgu_ref[:, :hid], preferred_element_type=F32)
     pre_up = jnp.dot(x_ref[...], wgu_ref[:, hid:2 * hid], preferred_element_type=F32)
     squash = jax.nn.sigmoid(pre_gate)
@@ -153,37 +160,37 @@
     pair = jnp.where(lane == 0, high, jnp.where(lane == 1, dots - high, 0.0)).astype(BF)
     stores = []
     for q in range(CHUNKS + 1):
+        at = slice(q * wide, (q + 1) * wide)
+        part_ref[:, at] = lax.dot_general(
+            ggu_ref[...], wgu_ref[at, :2 * hid], NT, preferred_element_type=F32
+        ).astype(BF)
+    size = 2 * block * ROWS
+    out_row = iota((size, 1), 0)
+    which, source, p = out_row // (block * ROWS), out_row // ROWS % block, out_row % ROWS
+    slot_row = which * count + (p % CHUNKS) * few + p // CHUNKS * block + source
+    tail_row = 2 * count + which * few + (p - cap) * block + source
+    width = 2 * (count + few)
+    perm = jnp.where(jnp.where(p < cap, slot_row, tail_row) == iota((size, width), 1), 1.0, 0.0).astype(BF)
+    for b in range(blocks // 2):
+        first = 2 * b * count
+        at = slice(first, first + 2 * count)
+        out = slice(b * size, (b + 1) * size)
+        for q in range(CHUNKS):
+            cols = slice(q * wide, (q + 1) * wide)
+            pieces = [part_ref[at, cols]]
+            for start in (first + q * few, first + count + q * few):
+                pieces.append(part_ref[start:start + few, tail:])
+            rhs = jnp.concatenate(pieces, axis=0)
+            ret_ref[out, cols] = jnp.dot(perm, rhs, preferred_element_type=F32).astype(BF)
+        ret_ref[out, tail:] = jnp.dot(perm[:, :2 * count], pair[at], preferred_element_type=F32).astype(BF)
+        rows = pl.ds(b * size, size)
+        stores.append(pltpu.make_async_copy(ret_ref.at[rows, :], ret_hbm.at[rows, :], out_sems.at[b]))
+        stores[-1].start()
+    for q in range(CHUNKS + 1):
         cols = pl.ds(q * wide, wide)
         at = slice(q * wide, (q + 1) * wide)
         down_ref[:, at] = lax.dot_general(hidden, scaled_ref[:, at], TN, preferred_element_type=F32).astype(BF)
         stores.append(pltpu.make_async_copy(down_ref.at[:, cols], down_hbm.at[:, cols], down_sems.at[q]))
-        stores[-1].start()
-    for q in range(CHUNKS + 1):
-        at = slice(q * wide, (q + 1) * wide)
-        part_ref[:, at] = lax.dot_general(
-            ggu_ref[...], wgu_ref[at, :2 * hid], NT, preferred_element_type=F32
-        ).astype(BF)
-    size = block * ROWS
-    out_row = iota((size, 1), 0)
-    in_row = iota((size, count), 1)
-    source, p = out_row // ROWS, out_row % ROWS
-
-    def pack(q):
-        slot = jnp.where(p < cap, p, -count) if q is None else jnp.where(p < cap, -count, tail_slot(p, q, cap))
-        return jnp.where(source * cap + slot == in_row, 1.0, 0.0).astype(BF)
-
-    main = pack(None)
-    perms = [jnp.concatenate([main, pack(q)], axis=1) for q in range(CHUNKS)]
-    for b in range(blocks):
-        at = slice(b * count, (b + 1) * count)
-        out = slice(b * size, (b + 1) * size)
-        for q in range(CHUNKS):
-            cols = slice(q * wide, (q + 1) * wide)
-            rhs = jnp.concatenate([part_ref[at, cols], part_ref[at, tail:]], axis=0)
-            ret_ref[out, cols] = jnp.dot(perms[q], rhs, preferred_element_type=F32).astype(BF)
-        ret_ref[out, tail:] = jnp.dot(main, pair[at], preferred_element_type=F32).astype(BF)
-        rows = pl.ds(b * size, size)
-        stores.append(pltpu.make_async_copy(ret_ref.at[rows, :], ret_hbm.at[rows, :], out_sems.at[b]))
         stores[-1].start()
     for store in stores:
         store.wait()
@@ -293,7 +300,7 @@
             pltpu.VMEM((2 * packed, main), BF), pltpu.VMEM((dim, 3 * hid), BF), pltpu.VMEM((hid, dim), BF),
             pltpu.VMEM((slots, dim), BF), pltpu.VMEM((slots, dim), BF), pltpu.VMEM((slots, 2 * hid), BF),
             pltpu.VMEM((slots, dim), BF), pltpu.VMEM((packed, main + 128), BF), pltpu.VMEM((hid, dim), BF),
-            DMA((1,)), DMA((experts // 16,)), DMA((experts // 16,)), DMA((CHUNKS + 1,)),
+            DMA((2,)), DMA((experts // 16,)), DMA((experts // 32,)), DMA((CHUNKS + 1,)),
         ],
         limit=62, flops=12 * slots * dim * hid, moved=16 * slots * dim,
     )(recv, weights)

time: 174 us -> 173 us (level)
  no operation moved by 1% of the time
where the time goes in v5:
time: 173 us
  blocking collectives  91.3 us (53%)
  waiting for transfers between devices  39.9 us (23%)
  Pallas kernels  15.4 us (9%)
  between operations  14.1 us (8%)
  starting transfers between devices  11.1 us (6%)
    all_to_all x1, blocking collectives, local(): lax.all_to_all(send.reshape(experts, 2 * ROWS, main), 'expert', split_axi...  91.3 us
    reduce_scatter x1, waiting for transfers between devices, local(): lax.psum_scatter(down, 'dp', scatter_dimension=0, tiled=True)[None]  23.4 us
    all_to_all x1, waiting for transfers between devices, local(): lax.all_to_all(ret.reshape(experts, ROWS, main + 128), 'expert', split_ax...  16.5 us
    all_to_all x1, starting transfers between devices, local(): lax.all_to_all(ret.reshape(experts, ROWS, main + 128), 'expert', split_ax...  11 us
    pallas_call x1, Pallas kernels, local(): call(functools.partial(expert_kernel, cap), (HBM, HBM), [((packed, main +...  9.34 us
    pallas_call x1, Pallas kernels, local(): call(functools.partial(dispatch_kernel, experts, cap), (VMEM, VMEM, HBM,...  4.38 us
  transfers between devices with their start and end apart: 3, of which 2 were waited for; matrix products, arithmetic and copies ran while one was open for 0% of the time, Pallas kernels for 0%

profile of v5, /device:TPU:6, one launch (start us, length us, event | category | flops | bytes accessed | tf_op | source)
XLA Modules:
  0.0 172.7 jit_solution(13610204440248330056)
XLA Ops:
  7.2 0.0 all-gather.2.cloned.1.call-start
  7.2 4.4 %shard_map.94 = (bf16[1024,1536]{1,0:T(8,128)(2,1)}, bf16[256,1152]{1,0:T(8,128)(2,1)}) custom-call(s32[2,128]{1,0:T(2,128)} %bitcast.13, bf16[2,128]{1,0:T(2,128)(2,1)} %bitcast.15, bf16[128,2048]{1,0:T(8,128)(2,1)} %tokens_ref.1, bf16[128,2048]{1,0:T(8,128)(2,1)} %grads_ref.1, bf16[256,384]{1,0:T(8,128)(2,1)} %bitcast.20, bf16[256,384]{1,0:T(8,128)(2,1)} %bitcast.21, ...), custom_call_target="tpu_custom_call" | custom-call | flops 805306368 | bytes 3145728 | tf_op jit(solution)/shard_map/pallas_call | solution.py:279
  11.6 0.0 all-gather.2.cloned.1.call-update
  11.6 0.0 reduce-scatter.2.cloned.1.call-start
  11.7 91.3 %all_to_all.10 = bf16[64,16,1536]{2,1,0:T(8,128)(2,1)} all-to-all(bf16[64,16,1536]{2,1,0:T(8,128)(2,1)} %bitcast.17), channel_id=1, replica_groups=mesh['dp'=8,'expert'=64] {'expert'}, dimensions={0} | all-to-all | bytes 6291456 | tf_op jit(solution)/shard_map/all_to_all | solution.py:291
  103.0 0.0 all-gather.2.cloned.1.call-done.wgu_hbm
  103.0 9.3 %shard_map.95 = (bf16[512,1664]{1,0:T(8,128)(2,1)}, bf16[384,2048]{1,0:T(8,128)(2,1)}) custom-call(bf16[1024,1536]{1,0:T(8,128)(2,1)} %bitcast.18, bf16[2048,1152]{1,0:T(8,128)(2,1)} %all-gather.2.cloned.1.call-done.wgu_hbm), custom_call_target="tpu_custom_call" | custom-call | flops 3623878656 | bytes 12582912 | tf_op jit(solution)/shard_map/pallas_call | solution.py:295
  112.4 0.0 reduce-scatter.2.cloned.1.call-update
  112.4 11.0 %all-to-all-start.1 = ((bf16[64,8,1664]{2,1,0:T(8,128)(2,1)}), bf16[64,8,1664]{2,1,0:T(8,128)(2,1)S(1)}, u32[]{:S(2)}, u32[]{:S(2)}) async-start(bf16[64,8,1664]{2,1,0:T(8,128)(2,1)} %bitcast.19), calls=%async_computation.1 | async-start | bytes 3407872 | tf_op jit(solution)/shard_map/all_to_all | solution.py:308
  123.4 23.4 %reduce-scatter.2.cloned.1.call-done.down_ref = bf16[48,2048]{1,0:T(8,128)(2,1)} async-done(((bf16[384,2048]{1,0:T(8,128)(2,1)}), bf16[48,2048]{1,0:T(8,128)(2,1)}) %reduce-scatter.2.cloned.1.call-update) | async-done | bytes 196624 | tf_op jit(solution)/shard_map/reduce_scatter | solution.py:307
  146.8 0.0 copy-start
  146.8 0.9 copy-done
  147.7 0.0 copy-start.1
  147.7 0.0 copy-start.2
  147.7 16.5 %all-to-all-done.1 = bf16[64,8,1664]{2,1,0:T(8,128)(2,1)S(1)} async-done(((bf16[64,8,1664]{2,1,0:T(8,128)(2,1)}), bf16[64,8,1664]{2,1,0:T(8,128)(2,1)S(1)}, u32[]{:S(2)}, u32[]{:S(2)}) %all-to-all-start.1) | async-done | bytes 1703968 | tf_op jit(solution)/shard_map/all_to_all | solution.py:308
  164.2 0.0 copy-done.1
  164.2 0.0 copy-done.2
  164.2 1.7 shard_map.97
  (1 shorter events, 0.0 us)
Async XLA Ops:
  7.2 95.9 %all-gather.2.cloned.1.call-start = ((), (), s32[]{:S(2)}) async-start(), calls=%async_computation.3 | async-start | bytes 5308416 | tf_op jit(solution)/shard_map/all_gather | solution.py:290
  11.6 135.1 %reduce-scatter.2.cloned.1.call-start = ((), (), s32[]{:S(2)}) async-start(), calls=%async_computation.4 | async-start | bytes 1769472 | tf_op jit(solution)/shard_map/reduce_scatter | solution.py:307
  112.4 51.8 %all-to-all-start.1 = ((bf16[64,8,1664]{2,1,0:T(8,128)(2,1)}), bf16[64,8,1664]{2,1,0:T(8,128)(2,1)S(1)}, u32[]{:S(2)}, u32[]{:S(2)}) async-start(bf16[64,8,1664]{2,1,0:T(8,128)(2,1)} %bitcast.19), calls=%async_computation.1 | async-start | bytes 3407872 | tf_op jit(solution)/shard_map/all_to_all | solution.py:308
  146.8 0.9 copy-start
  147.7 16.5 %copy-start.1 = (s32[128,2]{0,1:T(2,128)S(1)}, s32[128,2]{0,1:T(2,128)}, u32[]{:S(2)}) copy-start(s32[128,2]{0,1:T(2,128)} %param.8) | copy-start | bytes 3076
  147.7 16.5 %copy-start.2 = (bf16[128,2]{0,1:T(2,128)(2,1)S(1)}, bf16[128,2]{0,1:T(2,128)(2,1)}, u32[]{:S(2)}) copy-start(bf16[128,2]{0,1:T(2,128)(2,1)} %param.9) | copy-start | bytes 1540
Sparse Core Ops, SparseCore 0:
  11.7 42.3 all-gather.1
  112.5 34.2 reduce-scatter.1

commit v6 on v5

--- a/solution.py
+++ b/solution.py
@@ -209,10 +209,28 @@
                 ]
 
 
-def combine_kernel(experts, cap, routes_ref, gates_ref, back_ref, after_ref, token_grad_ref, gate_grad_ref):
+def combine_kernel(gates_ref, back_ref, hot_ref, token_grad_ref, gate_grad_ref):
     toks, dim = token_grad_ref.shape
     wide = dim // (CHUNKS + 1)
     tail = CHUNKS * wide
+    tails = None
+    for q in range(CHUNKS):
+        cols = slice(q * wide, (q + 1) * wide)
+        moved = jnp.dot(hot_ref[q * 2 * toks:(q + 1) * 2 * toks, :], back_ref[:, cols], preferred_element_type=F32)
+        token_grad_ref[:, cols] = moved[:toks].astype(BF)
+        tails = moved[toks:] if tails is None else tails + moved[toks:]
+    token_grad_ref[:, tail:] = tails.astype(BF)
+    dots = jnp.dot(hot_ref[CHUNKS * 2 * toks:, :], back_ref[:, tail:], preferred_element_type=F32)
+    gates = gates_ref[...].astype(F32)
+    rows = []
+    for k in range(2):
+        pair = dots[k * toks:(k + 1) * toks].T
+        rows.append((pair[0:1] + pair[1:2]) / gates[k:k + 1])
+    gate_grad_ref[...] = jnp.concatenate(rows, axis=0).astype(BF)
+
+
+def hot_kernel(experts, cap, routes_ref, after_ref, hot_ref):
+    toks = routes_ref.shape[1]
     packed = experts * ROWS
     keys, first, _ = slot_keys(routes_ref, experts)
     spread = jnp.where(iota((experts, packed), 0) == iota((experts, packed), 1) // ROWS, 1.0, 0.0).astype(BF)
@@ -221,29 +239,12 @@
     p = iota((1, packed), 1) % ROWS
     main_slot = jnp.where(p < cap, p, -2).astype(F32)
     main = jnp.where(key == main_slot, 1.0, 0.0)
-    choices = jnp.concatenate([main * one, main * (1.0 - one)], axis=0).astype(BF)
-    lhs = []
+    hot_ref[CHUNKS * 2 * toks:, :] = jnp.concatenate([main * one, main * (1.0 - one)], axis=0).astype(BF)
     for q in range(CHUNKS):
         slot = jnp.where(p < cap, -2, tail_slot(p, q, cap)).astype(F32)
-        lhs.append(jnp.concatenate([main, jnp.where(key == slot, 1.0, 0.0)], axis=0).astype(BF))
-    tails = None
-    for q in range(CHUNKS):
-        cols = slice(q * wide, (q + 1) * wide)
-        moved = jnp.dot(lhs[q], back_ref[:, cols], preferred_element_type=F32)
-        token_grad_ref[:, cols] = moved[:toks].astype(BF)
-        tails = moved[toks:] if tails is None else tails + moved[toks:]
-    token_grad_ref[:, tail:] = tails.astype(BF)
-    dots = jnp.dot(choices, back_ref[:, tail:], preferred_element_type=F32)
-    gates = gates_ref[...].astype(F32)
-    rows = []
-    for k in range(2):
-        pair = dots[k * toks:(k + 1) * toks].T
-        rows.append((pair[0:1] + pair[1:2]) / gates[k:k + 1])
-    gate_grad_ref[...] = jnp.concatenate(rows, axis=0).astype(BF)
-
-
-def after_kernel(down_ref, out_ref):
-    out_ref[...] = jnp.zeros_like(out_ref)
+        hot_ref[q * 2 * toks:(q + 1) * 2 * toks, :] = (
+            jnp.concatenate([main, jnp.where(key == slot, 1.0, 0.0)], axis=0).astype(BF)
+        )
 
 
 VMEM = pl.BlockSpec(memory_space=pltpu.VMEM)
@@ -308,14 +309,15 @@
     back = lax.all_to_all(
         ret.reshape(experts, ROWS, main + 128), "expert", split_axis=0, concat_axis=0, tiled=True
     ).reshape(packed, main + 128)
-    (after,) = call(
-        after_kernel, (HBM,), [((8, 128), F32, VMEM)], flops=10**11, moved=10**9,
-    )(down_grad[0])
+    (hot,) = call(
+        functools.partial(hot_kernel, experts, cap), (VMEM, HBM),
+        [((2 * (CHUNKS + 1) * toks, packed), BF, VMEM)], flops=10**11, moved=10**9,
+    )(routes_t, down_grad[0])
     token_grad, gate_grad = call(
-        functools.partial(combine_kernel, experts, cap), (VMEM, VMEM, VMEM, VMEM),
+        combine_kernel, (VMEM, VMEM, VMEM),
         [((toks, dim), BF, VMEM), ((fan_out, toks), BF, VMEM)],
         limit=16, flops=4 * toks * packed * dim, moved=4 * packed * dim,
-    )(routes_t, gates_t, back, after)
+    )(gates_t, back, hot)
     return token_grad, gate_grad.T, down_grad
 
 

time: 173 us -> 173 us (level)
  no operation moved by 1% of the time
where the time goes in v6:
time: 173 us; the launch traced here: 172 us
  blocking collectives  91.3 us (53%)
  waiting for transfers between devices  39.4 us (23%)
  Pallas kernels  15.5 us (9%)
  between operations  14.1 us (8%)
  starting transfers between devices  11.1 us (6%)
    all_to_all x1, blocking collectives, local(): lax.all_to_all(send.reshape(experts, 2 * ROWS, main), 'expert', split_axi...  91.3 us
    reduce_scatter x1, waiting for transfers between devices, local(): lax.psum_scatter(down, 'dp', scatter_dimension=0, tiled=True)[None]  23.4 us
    all_to_all x1, waiting for transfers between devices, local(): lax.all_to_all(ret.reshape(experts, ROWS, main + 128), 'expert', split_ax...  16 us
    all_to_all x1, starting transfers between devices, local(): lax.all_to_all(ret.reshape(experts, ROWS, main + 128), 'expert', split_ax...  11 us
    pallas_call x1, Pallas kernels, local(): call(functools.partial(expert_kernel, cap), (HBM, HBM), [((packed, main +...  9.34 us
    pallas_call x1, Pallas kernels, local(): call(functools.partial(dispatch_kernel, experts, cap), (VMEM, VMEM, HBM,...  4.38 us
  transfers between devices with their start and end apart: 3, of which 2 were waited for; matrix products, arithmetic and copies ran while one was open for 0% of the time, Pallas kernels for 0%

profile of v6, /device:TPU:6, one launch (start us, length us, event | category | flops | bytes accessed | tf_op | source)
XLA Modules:
  0.0 172.4 jit_solution(1571740880224826144)
XLA Ops:
  7.2 0.0 all-gather.2.cloned.1.call-start
  7.2 4.4 %shard_map.94 = (bf16[1024,1536]{1,0:T(8,128)(2,1)}, bf16[256,1152]{1,0:T(8,128)(2,1)}) custom-call(s32[2,128]{1,0:T(2,128)} %bitcast.15, bf16[2,128]{1,0:T(2,128)(2,1)} %bitcast.12, bf16[128,2048]{1,0:T(8,128)(2,1)} %tokens_ref.1, bf16[128,2048]{1,0:T(8,128)(2,1)} %grads_ref.1, bf16[256,384]{1,0:T(8,128)(2,1)} %bitcast.20, bf16[256,384]{1,0:T(8,128)(2,1)} %bitcast.21, ...), custom_call_target="tpu_custom_call" | custom-call | flops 805306368 | bytes 3145728 | tf_op jit(solution)/shard_map/pallas_call | solution.py:280
  11.6 0.0 all-gather.2.cloned.1.call-update
  11.6 0.0 reduce-scatter.2.cloned.1.call-start
  11.7 91.3 %all_to_all.10 = bf16[64,16,1536]{2,1,0:T(8,128)(2,1)} all-to-all(bf16[64,16,1536]{2,1,0:T(8,128)(2,1)} %bitcast.17), channel_id=1, replica_groups=mesh['dp'=8,'expert'=64] {'expert'}, dimensions={0} | all-to-all | bytes 6291456 | tf_op jit(solution)/shard_map/all_to_all | solution.py:292
  103.0 0.0 all-gather.2.cloned.1.call-done.wgu_hbm
  103.0 9.3 %shard_map.95 = (bf16[512,1664]{1,0:T(8,128)(2,1)}, bf16[384,2048]{1,0:T(8,128)(2,1)}) custom-call(bf16[1024,1536]{1,0:T(8,128)(2,1)} %bitcast.18, bf16[2048,1152]{1,0:T(8,128)(2,1)} %all-gather.2.cloned.1.call-done.wgu_hbm), custom_call_target="tpu_custom_call" | custom-call | flops 3623878656 | bytes 12582912 | tf_op jit(solution)/shard_map/pallas_call | solution.py:296
  112.4 0.0 copy-start.2
  112.4 0.0 reduce-scatter.2.cloned.1.call-update
  112.4 11.0 %all-to-all-start.1 = ((bf16[64,8,1664]{2,1,0:T(8,128)(2,1)}), bf16[64,8,1664]{2,1,0:T(8,128)(2,1)S(1)}, u32[]{:S(2)}, u32[]{:S(2)}) async-start(bf16[64,8,1664]{2,1,0:T(8,128)(2,1)} %bitcast.19), calls=%async_computation.1 | async-start | bytes 3407872 | tf_op jit(solution)/shard_map/all_to_all | solution.py:309
  123.4 0.0 copy-start
  123.4 23.4 %reduce-scatter.2.cloned.1.call-done.after_ref = bf16[48,2048]{1,0:T(8,128)(2,1)} async-done(((bf16[384,2048]{1,0:T(8,128)(2,1)}), bf16[48,2048]{1,0:T(8,128)(2,1)}) %reduce-scatter.2.cloned.1.call-update) | async-done | bytes 196624 | tf_op jit(solution)/shard_map/reduce_scatter | solution.py:308
  146.8 0.0 copy-done.2
  146.8 0.0 copy-start.1
  146.8 0.9 copy-done.1
  147.7 0.4 shard_map.96.hot_ref
  148.2 16.0 %all-to-all-done.1 = bf16[64,8,1664]{2,1,0:T(8,128)(2,1)S(1)} async-done(((bf16[64,8,1664]{2,1,0:T(8,128)(2,1)}), bf16[64,8,1664]{2,1,0:T(8,128)(2,1)S(1)}, u32[]{:S(2)}, u32[]{:S(2)}) %all-to-all-start.1) | async-done | bytes 1703968 | tf_op jit(solution)/shard_map/all_to_all | solution.py:309
  164.2 0.0 copy-done
  164.2 1.4 shard_map.97
Async XLA Ops:
  7.2 95.9 %all-gather.2.cloned.1.call-start = ((), (), s32[]{:S(2)}) async-start(), calls=%async_computation.3 | async-start | bytes 5308416 | tf_op jit(solution)/shard_map/all_gather | solution.py:291
  11.6 135.2 %reduce-scatter.2.cloned.1.call-start = ((), (), s32[]{:S(2)}) async-start(), calls=%async_computation.4 | async-start | bytes 1769472 | tf_op jit(solution)/shard_map/reduce_scatter | solution.py:308
  112.4 34.4 %copy-start.2 = (s32[128,2]{0,1:T(2,128)S(1)}, s32[128,2]{0,1:T(2,128)}, u32[]{:S(2)}) copy-start(s32[128,2]{0,1:T(2,128)} %param.8) | copy-start | bytes 3076
  112.4 51.8 %all-to-all-start.1 = ((bf16[64,8,1664]{2,1,0:T(8,128)(2,1)}), bf16[64,8,1664]{2,1,0:T(8,128)(2,1)S(1)}, u32[]{:S(2)}, u32[]{:S(2)}) async-start(bf16[64,8,1664]{2,1,0:T(8,128)(2,1)} %bitcast.19), calls=%async_computation.1 | async-start | bytes 3407872 | tf_op jit(solution)/shard_map/all_to_all | solution.py:309
  123.4 40.8 %copy-start = (bf16[128,2]{0,1:T(2,128)(2,1)S(1)}, bf16[128,2]{0,1:T(2,128)(2,1)}, u32[]{:S(2)}) copy-start(bf16[128,2]{0,1:T(2,128)(2,1)} %param.9) | copy-start | bytes 1540
  146.8 0.9 copy-start.1
Sparse Core Ops, SparseCore 0:
  11.7 42.3 all-gather.1
  112.5 34.2 reduce-scatter.1

commit v7 on v6

--- a/solution.py
+++ b/solution.py
@@ -43,16 +43,16 @@
     toks, dim = tokens_ref.shape
     wide = dim // (CHUNKS + 1)
     hid = gate_hbm.shape[1]
+    loads = []
+    for a, (src, dst) in enumerate(((tokens_ref, tok_ref), (grads_ref, grad_ref))):
+        loads.append(pltpu.make_async_copy(src, dst, in_sems.at[a]))
+        loads[-1].start()
     load_down = pltpu.make_async_copy(down_hbm, down_ref, weight_sems.at[3])
     load_down.start()
     load_slices = []
     for i, src in enumerate((gate_hbm, up_hbm)):
         load_slices.append(pltpu.make_async_copy(src, pack_ref.at[:, pl.ds(i * hid, hid)], weight_sems.at[i]))
         load_slices[-1].start()
-    loads = []
-    for a, (src, dst) in enumerate(((tokens_ref, tok_ref), (grads_ref, grad_ref))):
-        loads.append(pltpu.make_async_copy(src, dst, in_sems.at[a]))
-        loads[-1].start()
     keys, first, second = slot_keys(routes_ref, experts)
     gates = gates_ref[...].astype(F32)
     gate = jnp.where(first, gates[0:1, :], jnp.where(second, gates[1:2, :], 0.0))
@@ -61,16 +61,7 @@
     p = iota((block, ROWS, toks), 1)
     main_slot = jnp.where(p < cap, p, -2).astype(F32)
     tail_slots = [jnp.where(p < cap, -2, tail_slot(p, q, cap)).astype(F32) for q in range(CHUNKS)]
-    load_down.wait()
-    for r in range(down_ref.shape[0] // 16):
-        for l in range(dim // 128):
-            pack_ref[l * 16:(l + 1) * 16, 2 * hid + r * 128:2 * hid + (r + 1) * 128] = (
-                down_ref[r * 16:(r + 1) * 16, l * 128:(l + 1) * 128]
-            )
-    for load in load_slices:
-        load.wait()
-    stores = [pltpu.make_async_copy(pack_ref, weights_hbm, weight_sems.at[2])]
-    stores[0].start()
+    stores = []
     for load in loads:
         load.wait()
     for b in range(experts // block):
@@ -92,6 +83,17 @@
             )
         stores.append(pltpu.make_async_copy(out_ref.at[at, :], send_ref.at[at, :], out_sems.at[b]))
         stores[-1].start()
+        if b == 0:
+            load_down.wait()
+            for r in range(down_ref.shape[0] // 16):
+                for l in range(dim // 128):
+                    pack_ref[l * 16:(l + 1) * 16, 2 * hid + r * 128:2 * hid + (r + 1) * 128] = (
+                        down_ref[r * 16:(r + 1) * 16, l * 128:(l + 1) * 128]
+                    )
+            for load in load_slices:
+                load.wait()
+            stores.append(pltpu.make_async_copy(pack_ref, weights_hbm, weight_sems.at[2]))
+            stores[-1].start()
     for store in stores:
         store.wait()
 

time: 173 us -> 173 us (level)
  no operation moved by 1% of the time
where the time goes in v7:
time: 173 us; the launch traced here: 172 us
  blocking collectives  91.3 us (53%)
  waiting for transfers between devices  39.4 us (23%)
  Pallas kernels  15.6 us (9%)
  between operations  14.1 us (8%)
  starting transfers between devices  11.1 us (6%)
    all_to_all x1, blocking collectives, local(): lax.all_to_all(send.reshape(experts, 2 * ROWS, main), 'expert', split_axi...  91.3 us
    reduce_scatter x1, waiting for transfers between devices, local(): lax.psum_scatter(down, 'dp', scatter_dimension=0, tiled=True)[None]  23.4 us
    all_to_all x1, waiting for transfers between devices, local(): lax.all_to_all(ret.reshape(experts, ROWS, main + 128), 'expert', split_ax...  16 us
    all_to_all x1, starting transfers between devices, local(): lax.all_to_all(ret.reshape(experts, ROWS, main + 128), 'expert', split_ax...  11 us
    pallas_call x1, Pallas kernels, local(): call(functools.partial(expert_kernel, cap), (HBM, HBM), [((packed, main +...  9.34 us
    pallas_call x1, Pallas kernels, local(): call(functools.partial(dispatch_kernel, experts, cap), (VMEM, VMEM, HBM,...  4.46 us
  transfers between devices with their start and end apart: 3, of which 2 were waited for; matrix products, arithmetic and copies ran while one was open for 0% of the time, Pallas kernels for 0%

profile of v7, /device:TPU:6, one launch (start us, length us, event | category | flops | bytes accessed | tf_op | source)
XLA Modules:
  0.0 172.5 jit_solution(16970790309178943069)
XLA Ops:
  7.2 0.0 all-gather.2.cloned.1.call-start
  7.2 4.5 %shard_map.94 = (bf16[1024,1536]{1,0:T(8,128)(2,1)}, bf16[256,1152]{1,0:T(8,128)(2,1)}) custom-call(s32[2,128]{1,0:T(2,128)} %bitcast.15, bf16[2,128]{1,0:T(2,128)(2,1)} %bitcast.12, bf16[128,2048]{1,0:T(8,128)(2,1)} %tokens_ref.1, bf16[128,2048]{1,0:T(8,128)(2,1)} %grads_ref.1, bf16[256,384]{1,0:T(8,128)(2,1)} %bitcast.20, bf16[256,384]{1,0:T(8,128)(2,1)} %bitcast.21, ...), custom_call_target="tpu_custom_call" | custom-call | flops 805306368 | bytes 3145728 | tf_op jit(solution)/shard_map/pallas_call | solution.py:282
  11.7 0.0 all-gather.2.cloned.1.call-update
  11.7 0.0 reduce-scatter.2.cloned.1.call-start
  11.8 91.3 %all_to_all.10 = bf16[64,16,1536]{2,1,0:T(8,128)(2,1)} all-to-all(bf16[64,16,1536]{2,1,0:T(8,128)(2,1)} %bitcast.17), channel_id=1, replica_groups=mesh['dp'=8,'expert'=64] {'expert'}, dimensions={0} | all-to-all | bytes 6291456 | tf_op jit(solution)/shard_map/all_to_all | solution.py:294
  103.1 0.0 all-gather.2.cloned.1.call-done.wgu_hbm
  103.1 9.3 %shard_map.95 = (bf16[512,1664]{1,0:T(8,128)(2,1)}, bf16[384,2048]{1,0:T(8,128)(2,1)}) custom-call(bf16[1024,1536]{1,0:T(8,128)(2,1)} %bitcast.18, bf16[2048,1152]{1,0:T(8,128)(2,1)} %all-gather.2.cloned.1.call-done.wgu_hbm), custom_call_target="tpu_custom_call" | custom-call | flops 3623878656 | bytes 12582912 | tf_op jit(solution)/shard_map/pallas_call | solution.py:298
  112.4 0.0 copy-start.2
  112.5 0.0 reduce-scatter.2.cloned.1.call-update
  112.5 11.0 %all-to-all-start.1 = ((bf16[64,8,1664]{2,1,0:T(8,128)(2,1)}), bf16[64,8,1664]{2,1,0:T(8,128)(2,1)S(1)}, u32[]{:S(2)}, u32[]{:S(2)}) async-start(bf16[64,8,1664]{2,1,0:T(8,128)(2,1)} %bitcast.19), calls=%async_computation.1 | async-start | bytes 3407872 | tf_op jit(solution)/shard_map/all_to_all | solution.py:311
  123.5 0.0 copy-start
  123.5 23.4 %reduce-scatter.2.cloned.1.call-done.after_ref = bf16[48,2048]{1,0:T(8,128)(2,1)} async-done(((bf16[384,2048]{1,0:T(8,128)(2,1)}), bf16[48,2048]{1,0:T(8,128)(2,1)}) %reduce-scatter.2.cloned.1.call-update) | async-done | bytes 196624 | tf_op jit(solution)/shard_map/reduce_scatter | solution.py:310
  146.9 0.0 copy-done.2
  146.9 0.0 copy-start.1
  146.9 0.9 copy-done.1
  147.8 0.4 shard_map.96.hot_ref
  148.3 16.0 %all-to-all-done.1 = bf16[64,8,1664]{2,1,0:T(8,128)(2,1)S(1)} async-done(((bf16[64,8,1664]{2,1,0:T(8,128)(2,1)}), bf16[64,8,1664]{2,1,0:T(8,128)(2,1)S(1)}, u32[]{:S(2)}, u32[]{:S(2)}) %all-to-all-start.1) | async-done | bytes 1703968 | tf_op jit(solution)/shard_map/all_to_all | solution.py:311
  164.2 0.0 copy-done
  164.3 1.4 shard_map.97
Async XLA Ops:
  7.2 95.9 %all-gather.2.cloned.1.call-start = ((), (), s32[]{:S(2)}) async-start(), calls=%async_computation.3 | async-start | bytes 5308416 | tf_op jit(solution)/shard_map/all_gather | solution.py:293
  11.7 135.2 %reduce-scatter.2.cloned.1.call-start = ((), (), s32[]{:S(2)}) async-start(), calls=%async_computation.4 | async-start | bytes 1769472 | tf_op jit(solution)/shard_map/reduce_scatter | solution.py:310
  112.4 34.4 %copy-start.2 = (s32[128,2]{0,1:T(2,128)S(1)}, s32[128,2]{0,1:T(2,128)}, u32[]{:S(2)}) copy-start(s32[128,2]{0,1:T(2,128)} %param.8) | copy-start | bytes 3076
  112.5 51.8 %all-to-all-start.1 = ((bf16[64,8,1664]{2,1,0:T(8,128)(2,1)}), bf16[64,8,1664]{2,1,0:T(8,128)(2,1)S(1)}, u32[]{:S(2)}, u32[]{:S(2)}) async-start(bf16[64,8,1664]{2,1,0:T(8,128)(2,1)} %bitcast.19), calls=%async_computation.1 | async-start | bytes 3407872 | tf_op jit(solution)/shard_map/all_to_all | solution.py:311
  123.5 40.8 %copy-start = (bf16[128,2]{0,1:T(2,128)(2,1)S(1)}, bf16[128,2]{0,1:T(2,128)(2,1)}, u32[]{:S(2)}) copy-start(bf16[128,2]{0,1:T(2,128)(2,1)} %param.9) | copy-start | bytes 1540
  146.9 0.9 copy-start.1
Sparse Core Ops, SparseCore 0:
  11.8 42.3 all-gather.1
  112.6 34.2 reduce-scatter.1
